TPU v7x, 256 devices: a whole 4x4x8 slice. The times are simulated.
256 devices in a mesh: lon: 16 (over x_hi, y, core), lat: 16 (over z, x_lo).
Axes of the slice: x: 4 (x_hi: 2, x_lo: 2; x = x_hi * 2 + x_lo), y: 4, z: 8, core: 2. Of those that a mesh axis runs over, the one named last changes fastest.
Arguments:
- input_first_batch: bfloat16 [2, 192, 192, 1024], P(None, 'lat', 'lon'), may hold values from -6 to 6
- input_second_batch: bfloat16 [2, 192, 192, 1024], P(None, 'lat', 'lon'), may hold values from -6 to 6
- cotangent_second_batch: bfloat16 [2, 192, 192, 1024], P(None, 'lat', 'lon'), may hold values from -6 to 6
- layer_norm_gain: float32 [1024], replicated, may hold values from 0.1 to 1.9
- query_key_value_weight: bfloat16 [1024, 3072], replicated, may hold values from -2 to 2
- output_projection_weight: bfloat16 [1024, 1024], replicated, may hold values from -0.1875 to 0.1875
- projection_adapter_down: bfloat16 [1024, 8], replicated, may hold values from -0.1875 to 0.1875
- projection_adapter_up: bfloat16 [8, 3072], replicated, may hold values from -2 to 2
- output_adapter_down: bfloat16 [1024, 8], replicated, may hold values from -0.1875 to 0.1875
- output_adapter_up: bfloat16 [8, 1024], replicated, may hold values from -2 to 2
Outputs:
- output_a: bfloat16 [2, 192, 192, 1024], P(None, 'lat', 'lon')
- input_grad_b: bfloat16 [2, 192, 192, 1024], P(None, 'lat', 'lon')
- grad_qkv_down: float32 [1024, 8], replicated
- grad_qkv_up: float32 [8, 3072], replicated
- grad_out_down: float32 [1024, 8], replicated
- grad_out_up: float32 [8, 1024], replicated
All inputs are finite; a program needn't handle non-finite values.
Results may differ from a plain program's by a relative error of at most 0.017.
Values may be sent and summed in bfloat16 or wider, within the bound.
No kernel may reach another device: no remote copies, remote signals or barrier semaphores. Data moves between devices by JAX's collectives and lax.ppermute only.
A program may use at most 128 MiB of HBM per device.

v0:
```python
import functools

import jax
import jax.numpy as jnp
from jax import lax
from jax.experimental import pallas as pl
from jax.experimental.pallas import tpu as pltpu
from jax.sharding import PartitionSpec as P

D = 1024
HD = 64
RANK = 8
TOK = 288
WIN = 144
HALF = 72
GH = 4
GW = GH * HD
NG = D // GW
GQ = GH * WIN
EPS = 1e-05
MASKED = -1e30
VMEM = 10 * 1024 * 1024
F32 = jnp.float32
BF16 = jnp.bfloat16


def nn(a, b):
    return jnp.dot(a, b, preferred_element_type=F32)


def nt(a, b):
    return lax.dot_general(a, b, (((1,), (1,)), ((), ())), preferred_element_type=F32)


def tn(a, b):
    return lax.dot_general(a, b, (((0,), (0,)), ((), ())), preferred_element_type=F32)


def layer_norm(tokens):
    average = jnp.mean(tokens, axis=-1, keepdims=True)
    centered = tokens - average
    variance = jnp.mean(centered * centered, axis=-1, keepdims=True)
    inv_std = lax.rsqrt(variance + EPS)
    return centered * inv_std, inv_std


def assemble(pieces, out_ref):
    at = 0
    for piece in pieces:
        rows = piece.shape[-2]
        out_ref[at : at + rows] = piece[...].astype(F32)
        at += rows


def take_apart(rows_ref, pieces):
    at = 0
    for piece in pieces:
        rows = piece.shape[-2]
        piece[...] = rows_ref[at : at + rows].astype(BF16)
        at += rows


def head_lanes(h):
    lane = lax.broadcasted_iota(jnp.int32, (1, GW), 1)
    return (lane >= h * HD) & (lane < (h + 1) * HD)


def spread_heads(a):
    zero = jnp.zeros_like(a)
    return jnp.concatenate([jnp.where(head_lanes(h), a, zero) for h in range(GH)], axis=0)


def gather_heads(a):
    out = a[:WIN]
    for h in range(1, GH):
        out = jnp.where(head_lanes(h), a[h * WIN : (h + 1) * WIN], out)
    return out


def pole_bias(polar):
    key = lax.broadcasted_iota(jnp.int32, (WIN, GQ), 0)
    query = lax.broadcasted_iota(jnp.int32, (WIN, GQ), 1)
    for h in range(1, GH):
        query = jnp.where(query >= WIN, query - WIN, query)
    apart = jnp.not_equal(key < HALF, query < HALF)
    return jnp.where(apart & (polar != 0), MASKED, 0.0)


def softmax_keys(q_blocks, k, bias_ref):
    scores = nt(k, q_blocks) + bias_ref[...]
    top = jnp.max(scores, axis=0, keepdims=True)
    p = jnp.exp(scores - top)
    return p * (1.0 / jnp.sum(p, axis=0, keepdims=True))


def project(normed, low, w_ref, up_ref, cols):
    return (nn(normed, w_ref[:, cols]) + nn(low, up_ref[:, cols])).astype(BF16)


def columns(i, g):
    return slice(i * D + g * GW, i * D + (g + 1) * GW)


def pack_kernel(*refs):
    sources, outs, fields, sems = refs[:3], refs[3:8], refs[8:11], refs[11]
    copies = [pltpu.make_async_copy(a, b, sems.at[i]) for i, (a, b) in enumerate(zip(sources, fields))]
    for copy in copies:
        copy.start()
    for copy in copies:
        copy.wait()
    *belows, corner, side = outs
    for i, field in enumerate(fields):
        below = belows[i].at[0]
        below[:72] = field[:6, 3:9].reshape(72, D)
        below[72:] = field[:6, 9:].reshape(36, D)
        corner[i] = field[:6, :3].reshape(36, D)
        side[i] = field[6:, :3].reshape(36, D)


def stage_kernel(*refs):
    sources, outs, sems = refs[:2], refs[2:4], refs[4]
    copies = [pltpu.make_async_copy(a, b, sems.at[i]) for i, (a, b) in enumerate(zip(sources, outs))]
    for copy in copies:
        copy.start()
    for copy in copies:
        copy.wait()


def pieces_of(field, below, corner, side):
    own0 = field[6:, 3:9].reshape(72, D)
    own1 = field[6:, 9:].reshape(36, D)
    return own0, below[...], corner[...], own1, side[...]


def attend_group(normed, low, wqkv_ref, pu_ref, bias_ref, g):
    q = project(normed, low, wqkv_ref, pu_ref, columns(0, g)) * 0.125
    k = project(normed, low, wqkv_ref, pu_ref, columns(1, g))
    v = project(normed, low, wqkv_ref, pu_ref, columns(2, g))
    contexts = []
    for w in range(2):
        rows = slice(w * WIN, (w + 1) * WIN)
        weights = softmax_keys(spread_heads(q[rows]), k[rows], bias_ref).astype(BF16)
        contexts.append(gather_heads(tn(weights, v[rows])).astype(BF16))
    return jnp.concatenate(contexts, axis=0)


def forward_first_kernel(
    polar_ref, field, below, corner, side, gain_ref, wqkv_ref, pd_ref, pu_ref,
    normed_ref, low_ref, context_ref, x_ref, bias_ref,
):
    assemble(pieces_of(field, below.at[0], corner.at[2], side.at[2]), x_ref)
    standard, _ = layer_norm(x_ref[...])
    normed = (standard * gain_ref[...]).astype(BF16)
    normed_ref[...] = normed
    low = nt(normed, pd_ref[...]).astype(BF16)
    low_ref[...] = low
    bias_ref[...] = pole_bias(polar_ref[0])
    for g in range(NG // 2):
        context_ref[:, columns(0, g)] = attend_group(normed, low, wqkv_ref, pu_ref, bias_ref, g)


def forward_second_kernel(
    polar_ref, normed_ref, low_ref, context_ref, wqkv_ref, wo_ref, pu_ref, od_ref, ou_ref, below_b,
    corner_b, side_b, own0, below, corner, own1, side, rows_ref, bias_ref,
):
    bias_ref[...] = pole_bias(polar_ref[0])
    normed, low = normed_ref[...], low_ref[...]
    groups = [
        attend_group(normed, low, wqkv_ref, pu_ref, bias_ref, g) for g in range(NG // 2, NG)
    ]
    context = jnp.concatenate([context_ref[...], *groups], axis=1)
    low_out = nt(context, od_ref[...]).astype(BF16)
    rows_ref[...] = nn(context, wo_ref[...]) + nn(low_out, ou_ref[...])
    take_apart(rows_ref, [a.at[0] for a in (own0, below, corner, own1, side)])
    below[1] = below_b[...]
    corner[1] = corner_b[...]
    side[1] = side_b[...]


def encode_kernel(
    polar_ref, field, below, corner, side, gain_ref, wqkv_ref, pd_ref, pu_ref, od_ref,
    x_ref, normed_ref, lowt_ref, qkv_ref, soft_ref, context_ref, lowt_out_ref, bias_ref,
):
    assemble(pieces_of(field, below.at[0], corner.at[0], side.at[0]), x_ref)
    standard, _ = layer_norm(x_ref[...])
    normed = (standard * gain_ref[...]).astype(BF16)
    normed_ref[...] = normed
    low = nt(normed, pd_ref[...])
    lowt_ref[...] = low.T.astype(BF16)
    low = low.astype(BF16)
    bias_ref[...] = pole_bias(polar_ref[0])
    low_out = jnp.zeros((TOK, RANK), F32)
    for g in range(NG):
        q = project(normed, low, wqkv_ref, pu_ref, columns(0, g)) * 0.125
        k = project(normed, low, wqkv_ref, pu_ref, columns(1, g))
        v = project(normed, low, wqkv_ref, pu_ref, columns(2, g))
        for i, a in enumerate((q, k, v)):
            qkv_ref[:, columns(i, g)] = a
        contexts = []
        for w in range(2):
            rows = slice(w * WIN, (w + 1) * WIN)
            softmaxed = softmax_keys(spread_heads(q[rows]), k[rows], bias_ref)
            soft_ref[2 * g + w] = softmaxed
            contexts.append(gather_heads(tn(softmaxed.astype(BF16), v[rows])).astype(BF16))
        context = jnp.concatenate(contexts, axis=0)
        context_ref[:, columns(0, g)] = context
        low_out += nt(context, od_ref[:, columns(0, g)])
    lowt_out_ref[...] = low_out.T.astype(BF16)


def grads_kernel(
    field, below, corner, side, normed_ref, lowt_ref, qkv_ref, soft_ref, context_ref, lowt_out_ref,
    wo_ref, pu_ref, od_ref, ou_ref, gp_ref, clq_ref, grads_ref, rows_ref,
):
    assemble(pieces_of(field, below.at[0], corner.at[1], side.at[1]), rows_ref)
    cot = rows_ref[...].astype(BF16)
    clo = nt(cot, ou_ref[...])
    clot = clo.T.astype(BF16)
    clo = clo.astype(BF16)
    lowt = lowt_ref[...]
    cl = jnp.zeros((TOK, RANK), F32)
    for g in range(NG):
        own = columns(0, g)
        q, k, v = (qkv_ref[:, columns(i, g)] for i in range(3))
        grad_context = (nt(cot, wo_ref[own, :]) + nn(clo, od_ref[:, own])).astype(BF16)
        gqs, gks, gvs = [], [], []
        for w in range(2):
            rows = slice(w * WIN, (w + 1) * WIN)
            q_blocks, g_blocks = spread_heads(q[rows]), spread_heads(grad_context[rows])
            softmaxed = soft_ref[2 * g + w]
            grad_weights = nt(v[rows], g_blocks)
            inner = jnp.sum(grad_weights * softmaxed, axis=0, keepdims=True)
            grad_scores = (softmaxed * (grad_weights - inner)).astype(BF16)
            gqs.append((gather_heads(tn(grad_scores, k[rows])) * 0.125).astype(BF16))
            gks.append(nn(grad_scores, q_blocks).astype(BF16))
            gvs.append(nn(softmaxed.astype(BF16), g_blocks).astype(BF16))
        for i, parts in enumerate((gqs, gks, gvs)):
            gp = jnp.concatenate(parts, axis=0)
            gp_ref[:, columns(i, g)] = gp
            grads_ref[g, 8 * i : 8 * i + 8] = nn(lowt, gp)
            cl += nt(gp, pu_ref[:, columns(i, g)])
        grads_ref[g, 24:32] = nn(clot, context_ref[:, own])
    clq_ref[...] = cl.astype(BF16)
    down = nn(cl.T.astype(BF16), normed_ref[...])
    up = nn(lowt_out_ref[...], cot)
    for g in range(NG):
        grads_ref[g, 32:40] = down[:, g * GW : (g + 1) * GW]
        grads_ref[g, 40:48] = up[:, g * GW : (g + 1) * GW]


def input_grad_kernel(
    x_ref, gain_ref, gp_ref, wqkv_ref, clq_ref, pd_ref, o0, o1, o2, o3, o4, rows_ref
):
    standard, inv_std = layer_norm(x_ref[...])
    grad_normed = nt(gp_ref[...], wqkv_ref[...]) + nn(clq_ref[...], pd_ref[...])
    grad_hat = grad_normed * gain_ref[...]
    along = jnp.mean(grad_hat * standard, axis=-1, keepdims=True)
    mean = jnp.mean(grad_hat, axis=-1, keepdims=True)
    rows_ref[...] = inv_std * (grad_hat - mean - standard * along)
    take_apart(rows_ref, (o0, o1, o2, o3, o4))


def clip_kernel(first_ref, mine_ref, other_ref, qd_ref, qu_ref, od_ref, ou_ref):
    mine, other = mine_ref[...].astype(F32), other_ref[...].astype(F32)
    total = jnp.sum(jnp.sum(mine * mine, axis=(0, 1)) + jnp.sum(other * other, axis=(0, 1)))
    limit = jnp.sqrt(jnp.full((8, GW), 6.0 * D * RANK, F32))
    factor = jnp.minimum(1.0, limit / (jnp.sqrt(jnp.full((8, GW), total)) + 1e-06))
    is_first = first_ref[0] == 0
    for g in range(NG):
        own = mine[g % 2]
        far = other[g % 2]
        part = jnp.where(is_first, own, far) if g < 2 else jnp.where(is_first, far, own)
        cols = slice(g * GW, (g + 1) * GW)
        for i in range(3):
            qu_ref[:, columns(i, g)] = part[8 * i : 8 * i + 8] * factor
        od_ref[:, cols] = part[24:32] * factor
        qd_ref[:, cols] = part[32:40] * factor
        ou_ref[:, cols] = part[40:48] * factor


SMEM_SPEC = pl.BlockSpec(memory_space=pltpu.SMEM)
VMEM_SPEC = pl.BlockSpec(memory_space=pltpu.VMEM)
PIECES = (72, 108, 36, 36, 36)


def cost(us):
    return pl.CostEstimate(flops=us * 1000000000, bytes_accessed=4000000, transcendentals=0)


def call(kernel, name, us, scalars, arrays, outs, scratch):
    return pl.pallas_call(
        kernel,
        in_specs=[SMEM_SPEC] * len(scalars) + [VMEM_SPEC] * len(arrays),
        out_specs=[VMEM_SPEC] * len(outs),
        out_shape=[jax.ShapeDtypeStruct(shape, dtype) for shape, dtype in outs],
        scratch_shapes=scratch,
        compiler_params=pltpu.CompilerParams(vmem_limit_bytes=VMEM),
        cost_estimate=cost(us),
        name=name,
    )(*scalars, *arrays)


PIECE_OUTS = [((rows, D), BF16) for rows in PIECES]
ROWS_SCRATCH = pltpu.VMEM((TOK, D), F32)
BIAS_SCRATCH = pltpu.VMEM((WIN, GQ), F32)


def run_pack(x_b, cot, x_a):
    fields = [pltpu.with_memory_space_constraint(a, pltpu.HBM) for a in (x_b, cot, x_a)]
    return pl.pallas_call(
        pack_kernel,
        in_specs=[pl.BlockSpec(memory_space=pltpu.HBM)] * 3,
        out_specs=[VMEM_SPEC] * 5,
        out_shape=[
            jax.ShapeDtypeStruct(shape, BF16)
            for shape in ((1, 108, D), (1, 108, D), (1, 108, D), (3, 36, D), (3, 36, D))
        ],
        scratch_shapes=[
            *[pltpu.VMEM((12, 12, 2, D), BF16) for _ in range(3)],
            pltpu.SemaphoreType.DMA((3,)),
        ],
        compiler_params=pltpu.CompilerParams(vmem_limit_bytes=VMEM),
        cost_estimate=cost(20),
        name="pack",
    )(*fields)


def run_stage(wqkv, wo):
    return pl.pallas_call(
        stage_kernel,
        in_specs=[pl.BlockSpec(memory_space=pltpu.HBM)] * 2,
        out_specs=[VMEM_SPEC] * 2,
        out_shape=[jax.ShapeDtypeStruct(a.shape, BF16) for a in (wqkv, wo)],
        scratch_shapes=[pltpu.SemaphoreType.DMA((2,))],
        compiler_params=pltpu.CompilerParams(vmem_limit_bytes=VMEM),
        cost_estimate=cost(3),
        name="stage",
    )(*[pltpu.with_memory_space_constraint(a, pltpu.HBM) for a in (wqkv, wo)])


def run_forward_first(polar, field, halo, weights):
    gain, wqkv, _, pd, pu, _, _ = weights
    outs = [((TOK, D), BF16), ((TOK, RANK), BF16), ((TOK, D // 2), BF16)]
    arrays = [field, *halo, gain, wqkv, pd, pu]
    scratch = [ROWS_SCRATCH, BIAS_SCRATCH]
    return call(forward_first_kernel, "forward_first", 4, [polar], arrays, outs, scratch)


def run_forward_second(polar, saved, pieces_b, weights):
    _, wqkv, wo, _, pu, od, ou = weights
    outs = [((n, rows, D), BF16) for n, rows in ((1, 72), (2, 108), (2, 36), (1, 36), (2, 36))]
    arrays = [*saved, wqkv, wo, pu, od, ou, *pieces_b]
    scratch = [ROWS_SCRATCH, BIAS_SCRATCH]
    return call(forward_second_kernel, "forward_second", 4, [polar], arrays, outs, scratch)


def run_encode(polar, field, halo, weights):
    gain, wqkv, _, pd, pu, od, _ = weights
    outs = [
        ((TOK, D), F32),
        ((TOK, D), BF16),
        ((RANK, TOK), BF16),
        ((TOK, 3 * D), BF16),
        ((2 * NG, WIN, GQ), F32),
        ((TOK, D), BF16),
        ((RANK, TOK), BF16),
    ]
    arrays = [field, *halo, gain, wqkv, pd, pu, od]
    return call(encode_kernel, "encode", 7, [polar], arrays, outs, [BIAS_SCRATCH])


def run_grads(field, halo, saved, weights):
    _, _, wo, _, pu, od, ou = weights
    outs = [((TOK, 3 * D), BF16), ((TOK, RANK), BF16), ((NG, 48, GW), F32)]
    arrays = [field, *halo, *saved, wo, pu, od, ou]
    return call(grads_kernel, "grads", 7, [], arrays, outs, [ROWS_SCRATCH])


def run_input_grad(x, gp, clq, weights):
    gain, wqkv, _, pd, _, _, _ = weights
    return call(
        input_grad_kernel, "input_grad", 3, [], [x, gain, gp, wqkv, clq, pd], PIECE_OUTS, [ROWS_SCRATCH]
    )


def run_clip(first, mine, other):
    outs = [((RANK, n), F32) for n in (D, 3 * D, D, D)]
    return call(clip_kernel, "clip", 1, [first], [mine, other], outs, [])


def shifted(block, lon, lat):
    n_lon, n_lat = lax.axis_size("lon"), lax.axis_size("lat")
    route = [
        (((i + lon) % n_lon) * n_lat + (j + lat) % n_lat, i * n_lat + j)
        for i in range(n_lon)
        for j in range(n_lat)
    ]
    return lax.ppermute(block, ("lon", "lat"), route)


def add_back(field, own0, below, corner, own1, side):
    grid6 = lambda a: a.reshape(6, 6, 2, D)
    grid3 = lambda a: a.reshape(6, 3, 2, D)
    upper = jnp.concatenate([grid3(corner), grid6(below[:72]), grid3(below[72:])], axis=1)
    lower = jnp.concatenate([grid3(side), grid6(own0), grid3(own1)], axis=1)
    back = jnp.transpose(jnp.concatenate([upper, lower], axis=0), (2, 0, 1, 3))
    return (field.astype(F32) + back.astype(F32)).astype(BF16)


def partner(block, lon_bit, lat_bit):
    n_lon, n_lat = lax.axis_size("lon"), lax.axis_size("lat")
    route = [
        ((i ^ lon_bit) * n_lat + (j ^ lat_bit), i * n_lat + j) for i in range(n_lon) for j in range(n_lat)
    ]
    return lax.ppermute(block, ("lon", "lat"), route)


def exchange(total, pair, work=None, args=()):
    sent = total.astype(BF16)
    if work is None:
        return sent.astype(F32) + partner(sent, *pair).astype(F32), None
    sent, args = lax.optimization_barrier((sent, args))
    got = partner(sent, *pair)
    got, done = lax.optimization_barrier((got, work(*args)))
    return sent.astype(F32) + got.astype(F32), done


def per_device(input_a, input_b, cot_b, gain, wqkv, wo, pd, pu, od, ou):
    n_lon, n_lat = lax.axis_size("lon"), lax.axis_size("lat")
    polar = (lax.axis_index("lat") == n_lat - 1).astype(jnp.int32).reshape(1)

    x_b, cot, x_a = (jnp.transpose(field, (1, 2, 0, 3)) for field in (input_b, cot_b, input_a))
    below_x, below_cot, below_a, corner, side = run_pack(x_b, cot, x_a)
    wqkv, wo, below_x = lax.optimization_barrier((wqkv, wo, below_x))
    staged = run_stage(wqkv, wo)
    below_x = shifted(below_x, 0, 1)
    corner = shifted(corner, 1, 1)
    side = shifted(side, 1, 0)
    wqkv, wo, below_x, corner, side, below_cot = lax.optimization_barrier(
        (*staged, below_x, corner, side, below_cot)
    )
    weights = (gain.reshape(1, D), wqkv, wo, pd.T, pu, od.T, ou)
    rows_b, *saved = run_encode(polar, x_b, (below_x, corner, side), weights)
    below_cot = shifted(below_cot, 0, 1)
    saved, below_cot, below_a = lax.optimization_barrier((saved, below_cot, below_a))
    gp, clq, grads = run_grads(cot, (below_cot, corner, side), saved, weights)
    below_a = shifted(below_a, 0, 1)

    core = lax.rem(lax.axis_index("lon"), 2)
    halves = grads[:2], grads[2:]
    kept = jnp.where(core == 0, halves[0], halves[1])
    sent = jnp.where(core == 0, halves[1], halves[0]).astype(BF16)
    total = kept + partner(sent, 1, 0).astype(F32)

    pairs = [(2, 0), (0, 1), (4, 0), (8, 0), (0, 2), (0, 4), (0, 8)]
    pairs = [(a, b) for a, b in pairs if a < n_lon and b < n_lat]
    total, (own0_b, below_b, corner_b, own1_b, side_b) = exchange(
        total, pairs[0], lambda *a: run_input_grad(*a, weights), (rows_b, gp, clq)
    )
    total, saved = exchange(
        total,
        pairs[1],
        lambda *halo: run_forward_first(polar, x_a, halo, weights),
        (below_a, corner, side),
    )
    total, (own0_a, below, corner, own1_a, side) = exchange(
        total,
        pairs[2],
        lambda *a: run_forward_second(polar, a[:3], a[3:], weights),
        (*saved, below_b, corner_b, side_b),
    )
    below = shifted(below, 0, -1)
    corner = shifted(corner, -1, -1)
    side = shifted(side, -1, 0)
    for pair in pairs[3:-1]:
        total = exchange(total, pair)[0]
    total, (output_a, input_grad_b) = exchange(
        total,
        pairs[-1],
        lambda below, corner, side: (
            add_back(input_a, own0_a, below[0], corner[0], own1_a, side[0]),
            add_back(cot_b, own0_b, below[1], corner[1], own1_b, side[1]),
        ),
        (below, corner, side),
    )
    total = total.astype(BF16)
    qd, qu, od_grad, ou_grad = run_clip(core.reshape(1), total, partner(total, 1, 0))
    return output_a, input_grad_b, qd.T, qu, od_grad.T, ou_grad


def solution(mesh):
    field = P(None, "lat", "lon", None)
    return jax.shard_map(
        per_device,
        mesh=mesh,
        in_specs=(field,) * 3 + (P(),) * 7,
        out_specs=(field, field, P(), P(), P(), P()),
        check_vma=False,
    )
```

profile of v0, /device:TPU:1, one launch (start us, length us, event | category | flops | bytes accessed | tf_op | source)
XLA Modules:
  0.0 93.7 jit_solution(457408023459252442)
XLA Ops:
  0.6 1.6 %pack.1 = (bf16[1,108,1024]{2,1,0:T(8,128)(2,1)S(1)}, bf16[1,108,1024]{2,1,0:T(8,128)(2,1)S(1)}, bf16[1,108,1024]{2,1,0:T(8,128)(2,1)S(1)}, bf16[3,36,1024]{2,1,0:T(8,128)(2,1)S(1)}, bf16[3,36,1024]{2,1,0:T(8,128)(2,1)S(1)}) custom-call(bf16[12,12,2,1024]{3,2,1,0:T(2,128)(2,1)} %bitcast.22, bf16[12,12,2,1024]{3,2,1,0:T(2,128)(2,1)} %bitcast.18, ...), custom_call_target="tpu_custom_call" | custom-call | flops 20000000000 | bytes 4000000 | tf_op jit(solution)/shard_map/pack/pallas_call | solution.py:310
  2.2 7.4 %collective-permute-start = (bf16[1,108,1024]{2,1,0:T(8,128)(2,1)S(1)}, bf16[1,108,1024]{2,1,0:T(8,128)(2,1)S(1)}, u32[]{:S(2)}, u32[]{:S(2)}) collective-permute-start(bf16[1,108,1024]{2,1,0:T(8,128)(2,1)S(1)} %get-tuple-element.100), channel_id=1, source_target_pairs={{1,0},{2,1},{3,2},{4,3},{5,4},{6,5},{7,6},{8,7},{9,8},{10,9},{11,1... | collective-permute-start | bytes 663560 | tf_op jit(solution)/shard_map/ppermute | solution.py:398
  9.6 1.1 %collective-permute-start.1 = (bf16[3,36,1024]{2,1,0:T(8,128)(2,1)S(1)}, bf16[3,36,1024]{2,1,0:T(8,128)(2,1)S(1)}, u32[]{:S(2)}, u32[]{:S(2)}) collective-permute-start(bf16[3,36,1024]{2,1,0:T(8,128)(2,1)S(1)} %get-tuple-element.101), channel_id=1, source_target_pairs={{17,0},{18,1},{19,2},{20,3},{21,4},{22,5},{23,6},{24,7},{25,8},{26... | collective-permute-start | bytes 663560 | tf_op jit(solution)/shard_map/ppermute | solution.py:398
  10.7 3.6 %collective-permute-start.2 = (bf16[3,36,1024]{2,1,0:T(8,128)(2,1)S(1)}, bf16[3,36,1024]{2,1,0:T(8,128)(2,1)S(1)}, u32[]{:S(2)}, u32[]{:S(2)}) collective-permute-start(bf16[3,36,1024]{2,1,0:T(8,128)(2,1)S(1)} %get-tuple-element.102), channel_id=1, source_target_pairs={{16,0},{17,1},{18,2},{19,3},{20,4},{21,5},{22,6},{23,7},{24,8},{25... | collective-permute-start | bytes 663560 | tf_op jit(solution)/shard_map/ppermute | solution.py:398
  14.3 0.0 copy-start.2
  14.3 0.0 copy-start.3
  14.3 0.0 copy-start.4
  14.3 0.0 copy-start.7
  14.3 3.5 %stage.1 = (bf16[1024,3072]{1,0:T(8,128)(2,1)S(1)}, bf16[1024,1024]{1,0:T(8,128)(2,1)S(1)}) custom-call(bf16[1024,3072]{1,0:T(8,128)(2,1)} %refs_0_, bf16[1024,1024]{1,0:T(8,128)(2,1)} %refs_1_), custom_call_target="tpu_custom_call" | custom-call | flops 3000000000 | bytes 4000000 | tf_op jit(solution)/shard_map/stage/pallas_call | solution.py:329
  17.8 0.0 collective-permute-done.below
  17.8 1.4 %collective-permute-done.1.corner = bf16[3,36,1024]{2,1,0:T(8,128)(2,1)S(1)} collective-permute-done((bf16[3,36,1024]{2,1,0:T(8,128)(2,1)S(1)}, bf16[3,36,1024]{2,1,0:T(8,128)(2,1)S(1)}, u32[]{:S(2)}, u32[]{:S(2)}) %collective-permute-start.1) | collective-permute-done | bytes 221216 | tf_op jit(solution)/shard_map/ppermute | solution.py:398
  19.2 0.0 collective-permute-done.2.side
  19.2 6.2 %collective-permute-start.3 = (bf16[1,108,1024]{2,1,0:T(8,128)(2,1)S(1)}, bf16[1,108,1024]{2,1,0:T(8,128)(2,1)S(1)}, u32[]{:S(2)}, u32[]{:S(2)}) collective-permute-start(bf16[1,108,1024]{2,1,0:T(8,128)(2,1)S(1)} %get-tuple-element.114), channel_id=1, source_target_pairs={{1,0},{2,1},{3,2},{4,3},{5,4},{6,5},{7,6},{8,7},{9,8},{10,9},{11,1... | collective-permute-start | bytes 663560 | tf_op jit(solution)/shard_map/ppermute | solution.py:398
  25.3 0.0 copy-done.2
  25.3 0.0 copy-done.3
  25.4 0.0 copy-done.4
  25.4 0.0 copy-done.5
  25.4 0.0 copy-done.7
  25.4 0.0 copy-start
  25.4 0.0 copy-start.6
  25.4 6.5 %encode.1 = (f32[288,1024]{1,0:T(8,128)S(1)}, bf16[288,1024]{1,0:T(8,128)(2,1)S(1)}, bf16[8,288]{1,0:T(8,128)(2,1)S(1)}, bf16[288,3072]{1,0:T(8,128)(2,1)S(1)}, ...) custom-call(s32[1]{0:T(128)} %bitcast.1.polar_ref, ...), custom_call_target="tpu_custom_call" | custom-call | flops 7000000000 | bytes 4000000 | tf_op jit(solution)/shard_map/encode/pallas_call | solution.py:291
  31.9 0.0 collective-permute-done.3.below
  31.9 0.0 copy-done
  31.9 0.0 copy-done.6
  31.9 7.1 %grads.1 = (bf16[288,3072]{1,0:T(8,128)(2,1)S(1)}, bf16[288,8]{1,0:T(8,128)(2,1)S(1)}, f32[4,48,256]{2,1,0:T(8,128)S(1)}) custom-call(bf16[12,12,2,1024]{3,2,1,0:T(2,128)(2,1)S(1)} %bitcast.19, bf16[1,108,1024]{2,1,0:T(8,128)(2,1)S(1)} %collective-permute-done.3.below, bf16[3,36,1024]{2,1,0:T(8,128)(2,1)S(1)} %collective-permute-done.1.corner, ...), custom_call_target="tpu_custom_call" | custom-call | flops 7000000000 | bytes 4000000 | tf_op jit(solution)/shard_map/grads/pallas_call | solution.py:291
  39.1 0.1 collective-permute-start.4
  39.2 1.9 %collective-permute-start.6 = (bf16[1,108,1024]{2,1,0:T(8,128)(2,1)S(1)}, bf16[1,108,1024]{2,1,0:T(8,128)(2,1)S(1)}, u32[]{:S(2)}, u32[]{:S(2)}) collective-permute-start(bf16[1,108,1024]{2,1,0:T(8,128)(2,1)S(1)} %get-tuple-element.138), channel_id=1, source_target_pairs={{1,0},{2,1},{3,2},{4,3},{5,4},{6,5},{7,6},{8,7},{9,8},{10,9},{11,1... | collective-permute-start | bytes 663560 | tf_op jit(solution)/shard_map/ppermute | solution.py:398
  41.1 0.0 collective-permute-done.4
  41.1 0.0 copy-start.1
  41.1 1.6 %collective-permute-start.5 = (bf16[2,48,256]{2,1,0:T(8,128)(2,1)S(1)}, bf16[2,48,256]{2,1,0:T(8,128)(2,1)S(1)}, u32[]{:S(2)}, u32[]{:S(2)}) collective-permute-start(bf16[2,48,256]{2,1,0:T(8,128)(2,1)S(1)} %add_convert_fusion.7), channel_id=1, source_target_pairs={{32,0},{33,1},{34,2},{35,3},{36,4},{37,5},{38,6},{39,7},{40,8},{41... | collective-permute-start | bytes 147464 | tf_op jit(solution)/shard_map/ppermute | solution.py:415
  42.7 2.4 %input_grad.1 = (bf16[72,1024]{1,0:T(8,128)(2,1)S(1)}, bf16[108,1024]{1,0:T(8,128)(2,1)S(1)}, bf16[36,1024]{1,0:T(8,128)(2,1)S(1)}, bf16[36,1024]{1,0:T(8,128)(2,1)S(1)}, bf16[36,1024]{1,0:T(8,128)(2,1)S(1)}) custom-call(f32[288,1024]{1,0:T(8,128)S(1)} %get-tuple-element.129.x_ref, f32[1,1024]{1,0:T(1,128)S(1)} %bitcast.31, ...), custom_call_target="tpu_custom_call" | custom-call | flops 3000000000 | bytes 4000000 | tf_op jit(solution)/shard_map/input_grad/pallas_call | solution.py:291
  45.2 0.0 collective-permute-done.5
  45.2 0.8 collective-permute-done.6.below
  46.0 0.0 collective-permute-start.7
  46.0 0.0 copy-done.1
  46.0 3.3 %forward_first.1 = (bf16[288,1024]{1,0:T(8,128)(2,1)S(1)}, bf16[288,8]{1,0:T(8,128)(2,1)S(1)}, bf16[288,512]{1,0:T(8,128)(2,1)S(1)}) custom-call(s32[1]{0:T(128)} %bitcast.1.polar_ref, bf16[12,12,2,1024]{3,2,1,0:T(2,128)(2,1)S(1)} %bitcast.21, bf16[1,108,1024]{2,1,0:T(8,128)(2,1)S(1)} %collective-permute-done.6.below, ...), custom_call_target="tpu_custom_call" | custom-call | flops 4000000000 | bytes 4000000 | tf_op jit(solution)/shard_map/forward_first/pallas_call | solution.py:291
  49.3 0.0 collective-permute-done.7
  49.4 2.7 %collective-permute-start.8 = (bf16[2,48,256]{2,1,0:T(8,128)(2,1)S(1)}, bf16[2,48,256]{2,1,0:T(8,128)(2,1)S(1)}, u32[]{:S(2)}, u32[]{:S(2)}) collective-permute-start(bf16[2,48,256]{2,1,0:T(8,128)(2,1)S(1)} %add_convert_fusion.5), channel_id=1, source_target_pairs={{64,0},{65,1},{66,2},{67,3},{68,4},{69,5},{70,6},{71,7},{72,8},{73... | collective-permute-start | bytes 147464 | tf_op jit(solution)/shard_map/ppermute | solution.py:415
  52.1 4.4 %forward_second.1 = (bf16[1,72,1024]{2,1,0:T(8,128)(2,1)S(1)}, bf16[2,108,1024]{2,1,0:T(8,128)(2,1)S(1)}, bf16[2,36,1024]{2,1,0:T(8,128)(2,1)S(1)}, bf16[1,36,10...) custom-call(s32[1]{0:T(128)} %bitcast.1.polar_ref, bf16[288,1024]{1,0:T(8,128)(2,1)S(1)} %get-tuple-element.154.normed_ref, ...), custom_call_target="tpu_custom_call" | custom-call | flops 4000000000 | bytes 4000000 | tf_op jit(solution)/shard_map/forward_second/pallas_call | solution.py:291
  56.5 0.0 collective-permute-done.8
  56.5 2.5 %collective-permute-start.9 = (bf16[2,48,256]{2,1,0:T(8,128)(2,1)S(1)}, bf16[2,48,256]{2,1,0:T(8,128)(2,1)S(1)}, u32[]{:S(2)}, u32[]{:S(2)}) collective-permute-start(bf16[2,48,256]{2,1,0:T(8,128)(2,1)S(1)} %add_convert_fusion.4), channel_id=1, source_target_pairs={{128,0},{129,1},{130,2},{131,3},{132,4},{133,5},{134,6},{135,7},{1... | collective-permute-start | bytes 147464 | tf_op jit(solution)/shard_map/ppermute | solution.py:415
  59.1 2.0 %collective-permute-done.9 = bf16[2,48,256]{2,1,0:T(8,128)(2,1)S(1)} collective-permute-done((bf16[2,48,256]{2,1,0:T(8,128)(2,1)S(1)}, bf16[2,48,256]{2,1,0:T(8,128)(2,1)S(1)}, u32[]{:S(2)}, u32[]{:S(2)}) %collective-permute-start.9) | collective-permute-done | bytes 49184 | tf_op jit(solution)/shard_map/ppermute | solution.py:415
  61.1 0.1 collective-permute-start.10
  61.2 1.5 %collective-permute-start.12 = (bf16[2,108,1024]{2,1,0:T(8,128)(2,1)S(1)}, bf16[2,108,1024]{2,1,0:T(8,128)(2,1)S(1)}, u32[]{:S(2)}, u32[]{:S(2)}) collective-permute-start(bf16[2,108,1024]{2,1,0:T(8,128)(2,1)S(1)} %get-tuple-element.166), channel_id=1, source_target_pairs={{15,0},{0,1},{1,2},{2,3},{3,4},{4,5},{5,6},{6,7},{7,8},{8,9},{9,10... | collective-permute-start | bytes 1327112 | tf_op jit(solution)/shard_map/ppermute | solution.py:398
  62.7 1.4 %collective-permute-done.10 = bf16[2,48,256]{2,1,0:T(8,128)(2,1)S(1)} collective-permute-done((bf16[2,48,256]{2,1,0:T(8,128)(2,1)S(1)}, bf16[2,48,256]{2,1,0:T(8,128)(2,1)S(1)}, u32[]{:S(2)}, u32[]{:S(2)}) %collective-permute-start.10) | collective-permute-done | bytes 49184 | tf_op jit(solution)/shard_map/ppermute | solution.py:415
  64.1 2.2 %collective-permute-start.11 = (bf16[2,48,256]{2,1,0:T(8,128)(2,1)S(1)}, bf16[2,48,256]{2,1,0:T(8,128)(2,1)S(1)}, u32[]{:S(2)}, u32[]{:S(2)}) collective-permute-start(bf16[2,48,256]{2,1,0:T(8,128)(2,1)S(1)} %add_convert_fusion.2), channel_id=1, source_target_pairs={{4,0},{5,1},{6,2},{7,3},{0,4},{1,5},{2,6},{3,7},{12,8},{13,9},{14,... | collective-permute-start | bytes 147464 | tf_op jit(solution)/shard_map/ppermute | solution.py:415
  66.3 0.1 reshape.64
  66.4 5.1 %collective-permute-start.13 = (bf16[2,36,1024]{2,1,0:T(8,128)(2,1)S(1)}, bf16[2,36,1024]{2,1,0:T(8,128)(2,1)S(1)}, u32[]{:S(2)}, u32[]{:S(2)}) collective-permute-start(bf16[2,36,1024]{2,1,0:T(8,128)(2,1)S(1)} %get-tuple-element.167), channel_id=1, source_target_pairs={{255,0},{240,1},{241,2},{242,3},{243,4},{244,5},{245,6},{246,7},{2... | collective-permute-start | bytes 442376 | tf_op jit(solution)/shard_map/ppermute | solution.py:398
  71.6 0.1 collective-permute-start.14
  71.7 0.1 reshape.60
  71.8 0.0 collective-permute-done.11
  71.8 8.4 %collective-permute-done.13 = bf16[2,36,1024]{2,1,0:T(8,128)(2,1)S(1)} collective-permute-done((bf16[2,36,1024]{2,1,0:T(8,128)(2,1)S(1)}, bf16[2,36,1024]{2,1,0:T(8,128)(2,1)S(1)}, u32[]{:S(2)}, u32[]{:S(2)}) %collective-permute-start.13) | collective-permute-done | bytes 147488 | tf_op jit(solution)/shard_map/ppermute | solution.py:398
  80.2 0.0 collective-permute-done.14
  80.2 0.0 collective-permute-done.12
  80.3 0.1 reshape.62
  80.4 0.9 %fusion.5 = (bf16[1,36,1024]{2,1,0:T(8,128)(2,1)S(1)}, bf16[1,36,1024]{2,1,0:T(8,128)(2,1)S(1)}) fusion(bf16[2,36,1024]{2,1,0:T(8,128)(2,1)} %collective-permute-done.14), kind=kLoop, calls=%fused_computation.16 | loop fusion | bytes 294912 | tf_op jit(solution)/shard_map/slice | solution.py:482
  81.5 0.1 reshape.58
  81.6 0.5 collective-permute-start.15
  82.1 1.9 %fusion = bf16[2,12,12,1024]{3,0,2,1:T(2,128)(2,1)} fusion(bf16[2,12,12,1024]{3,0,2,1:T(2,128)(2,1)S(1)} %copy-done, bf16[6,3,2,1024]{3,2,1,0:T(2,128)(2,1)S(1)} %reshape.65, bf16[6,6,2,1024]{3,2,1,0:T(2,128)(2,1)S(1)} %reshape.64, bf16[6,3,2,1024]{3,2,1,0:T(2,128)(2,1)S(1)} %reshape_squeeze.15, bf16[6,3,2,1024]{3,2,1,0:T(2,128)(2,1)S(1)} %reshape.63, ...), kind=kLoop, calls=%fused_computation.1 | loop fusion | flops 2654208 | bytes 1769472 | tf_op jit(solution)/shard_map/convert_element_type | solution.py:407
  84.0 1.9 %fusion.1 = bf16[2,12,12,1024]{3,0,2,1:T(2,128)(2,1)} fusion(bf16[2,12,12,1024]{3,0,2,1:T(2,128)(2,1)S(1)} %copy-done.1, bf16[6,3,2,1024]{3,2,1,0:T(2,128)(2,1)S(1)} %reshape.61, bf16[6,6,2,1024]{3,2,1,0:T(2,128)(2,1)S(1)} %reshape.60, bf16[6,3,2,1024]{3,2,1,0:T(2,128)(2,1)S(1)} %reshape_squeeze.13, bf16[6,3,2,1024]{3,2,1,0:T(2,128)(2,1)S(1)} %reshape.59, ...), kind=kLoop, calls=%fused_computation.3 | loop fusion | flops 2654208 | bytes 1769472 | tf_op jit(solution)/shard_map/convert_element_type | solution.py:407
  86.0 2.6 %collective-permute-done.15 = bf16[2,48,256]{2,1,0:T(8,128)(2,1)S(1)} collective-permute-done((bf16[2,48,256]{2,1,0:T(8,128)(2,1)S(1)}, bf16[2,48,256]{2,1,0:T(8,128)(2,1)S(1)}, u32[]{:S(2)}, u32[]{:S(2)}) %collective-permute-start.15) | collective-permute-done | bytes 49184 | tf_op jit(solution)/shard_map/ppermute | solution.py:415
  88.5 3.5 %collective-permute-start.16 = (bf16[2,48,256]{2,1,0:T(8,128)(2,1)S(1)}, bf16[2,48,256]{2,1,0:T(8,128)(2,1)S(1)}, u32[]{:S(2)}, u32[]{:S(2)}) collective-permute-start(bf16[2,48,256]{2,1,0:T(8,128)(2,1)S(1)} %add_convert_fusion.mine_ref), channel_id=1, source_target_pairs={{16,0},{17,1},{18,2},{19,3},{20,4},{21,5},{22,6},{23,7},{24,8},{25... | collective-permute-start | bytes 147464 | tf_op jit(solution)/shard_map/ppermute | solution.py:415
  92.0 0.9 collective-permute-done.16.other_ref
  92.9 0.8 clip.1
  (20 shorter events, 0.5 us)
Async XLA Ops:
  2.2 15.6 %collective-permute-start = (bf16[1,108,1024]{2,1,0:T(8,128)(2,1)S(1)}, bf16[1,108,1024]{2,1,0:T(8,128)(2,1)S(1)}, u32[]{:S(2)}, u32[]{:S(2)}) collective-permute-start(bf16[1,108,1024]{2,1,0:T(8,128)(2,1)S(1)} %get-tuple-element.100), channel_id=1, source_target_pairs={{1,0},{2,1},{3,2},{4,3},{5,4},{6,5},{7,6},{8,7},{9,8},{10,9},{11,1... | collective-permute-start | bytes 663560 | tf_op jit(solution)/shard_map/ppermute | solution.py:398
  9.6 9.5 %collective-permute-start.1 = (bf16[3,36,1024]{2,1,0:T(8,128)(2,1)S(1)}, bf16[3,36,1024]{2,1,0:T(8,128)(2,1)S(1)}, u32[]{:S(2)}, u32[]{:S(2)}) collective-permute-start(bf16[3,36,1024]{2,1,0:T(8,128)(2,1)S(1)} %get-tuple-element.101), channel_id=1, source_target_pairs={{17,0},{18,1},{19,2},{20,3},{21,4},{22,5},{23,6},{24,7},{25,8},{26... | collective-permute-start | bytes 663560 | tf_op jit(solution)/shard_map/ppermute | solution.py:398
  10.7 8.4 %collective-permute-start.2 = (bf16[3,36,1024]{2,1,0:T(8,128)(2,1)S(1)}, bf16[3,36,1024]{2,1,0:T(8,128)(2,1)S(1)}, u32[]{:S(2)}, u32[]{:S(2)}) collective-permute-start(bf16[3,36,1024]{2,1,0:T(8,128)(2,1)S(1)} %get-tuple-element.102), channel_id=1, source_target_pairs={{16,0},{17,1},{18,2},{19,3},{20,4},{21,5},{22,6},{23,7},{24,8},{25... | collective-permute-start | bytes 663560 | tf_op jit(solution)/shard_map/ppermute | solution.py:398
  14.3 11.1 %copy-start.2 = (bf16[2,12,12,1024]{3,0,2,1:T(2,128)(2,1)S(1)}, bf16[2,12,12,1024]{3,0,2,1:T(2,128)(2,1)}, u32[]{:S(2)}) copy-start(bf16[2,12,12,1024]{3,0,2,1:T(2,128)(2,1)} %param.11) | copy-start | bytes 1769476
  14.3 11.1 %copy-start.3 = (bf16[8,3072]{1,0:T(8,128)(2,1)S(1)}, bf16[8,3072]{1,0:T(8,128)(2,1)}, u32[]{:S(2)}) copy-start(bf16[8,3072]{1,0:T(8,128)(2,1)} %pu_ref.7) | copy-start | bytes 147460
  14.3 11.1 %copy-start.4 = (bf16[1024,8]{0,1:T(8,128)(2,1)S(1)}, bf16[1024,8]{0,1:T(8,128)(2,1)}, u32[]{:S(2)}) copy-start(bf16[1024,8]{0,1:T(8,128)(2,1)} %param.16) | copy-start | bytes 49156
  14.3 11.1 %copy-start.5 = (bf16[1024,8]{0,1:T(8,128)(2,1)S(1)}, bf16[1024,8]{0,1:T(8,128)(2,1)}, u32[]{:S(2)}) copy-start(bf16[1024,8]{0,1:T(8,128)(2,1)} %param.18) | copy-start | bytes 49156
  14.3 11.1 %copy-start.7 = (f32[1024]{0:T(1024)S(1)}, f32[1024]{0:T(1024)}, u32[]{:S(2)}) copy-start(f32[1024]{0:T(1024)} %param.13) | copy-start | bytes 12292
  19.2 12.7 %collective-permute-start.3 = (bf16[1,108,1024]{2,1,0:T(8,128)(2,1)S(1)}, bf16[1,108,1024]{2,1,0:T(8,128)(2,1)S(1)}, u32[]{:S(2)}, u32[]{:S(2)}) collective-permute-start(bf16[1,108,1024]{2,1,0:T(8,128)(2,1)S(1)} %get-tuple-element.114), channel_id=1, source_target_pairs={{1,0},{2,1},{3,2},{4,3},{5,4},{6,5},{7,6},{8,7},{9,8},{10,9},{11,1... | collective-permute-start | bytes 663560 | tf_op jit(solution)/shard_map/ppermute | solution.py:398
  25.4 6.5 %copy-start = (bf16[2,12,12,1024]{3,0,2,1:T(2,128)(2,1)S(1)}, bf16[2,12,12,1024]{3,0,2,1:T(2,128)(2,1)}, u32[]{:S(2)}) copy-start(bf16[2,12,12,1024]{3,0,2,1:T(2,128)(2,1)} %param.12) | copy-start | bytes 1769476
  25.4 6.5 %copy-start.6 = (bf16[8,1024]{1,0:T(8,128)(2,1)S(1)}, bf16[8,1024]{1,0:T(8,128)(2,1)}, u32[]{:S(2)}) copy-start(bf16[8,1024]{1,0:T(8,128)(2,1)} %ou_ref.3) | copy-start | bytes 49156
  39.1 2.0 %collective-permute-start.4 = (bf16[2,48,256]{2,1,0:T(8,128)(2,1)S(1)}, bf16[2,48,256]{2,1,0:T(8,128)(2,1)S(1)}, u32[]{:S(2)}, u32[]{:S(2)}) collective-permute-start(bf16[2,48,256]{2,1,0:T(8,128)(2,1)S(1)} %select_convert_fusion), channel_id=1, source_target_pairs={{16,0},{17,1},{18,2},{19,3},{20,4},{21,5},{22,6},{23,7},{24,8},{25... | collective-permute-start | bytes 147464 | tf_op jit(solution)/shard_map/ppermute | solution.py:415
  39.2 6.8 %collective-permute-start.6 = (bf16[1,108,1024]{2,1,0:T(8,128)(2,1)S(1)}, bf16[1,108,1024]{2,1,0:T(8,128)(2,1)S(1)}, u32[]{:S(2)}, u32[]{:S(2)}) collective-permute-start(bf16[1,108,1024]{2,1,0:T(8,128)(2,1)S(1)} %get-tuple-element.138), channel_id=1, source_target_pairs={{1,0},{2,1},{3,2},{4,3},{5,4},{6,5},{7,6},{8,7},{9,8},{10,9},{11,1... | collective-permute-start | bytes 663560 | tf_op jit(solution)/shard_map/ppermute | solution.py:398
  41.1 4.9 %copy-start.1 = (bf16[2,12,12,1024]{3,0,2,1:T(2,128)(2,1)S(1)}, bf16[2,12,12,1024]{3,0,2,1:T(2,128)(2,1)}, u32[]{:S(2)}) copy-start(bf16[2,12,12,1024]{3,0,2,1:T(2,128)(2,1)} %param.10) | copy-start | bytes 1769476
  41.1 4.0 %collective-permute-start.5 = (bf16[2,48,256]{2,1,0:T(8,128)(2,1)S(1)}, bf16[2,48,256]{2,1,0:T(8,128)(2,1)S(1)}, u32[]{:S(2)}, u32[]{:S(2)}) collective-permute-start(bf16[2,48,256]{2,1,0:T(8,128)(2,1)S(1)} %add_convert_fusion.7), channel_id=1, source_target_pairs={{32,0},{33,1},{34,2},{35,3},{36,4},{37,5},{38,6},{39,7},{40,8},{41... | collective-permute-start | bytes 147464 | tf_op jit(solution)/shard_map/ppermute | solution.py:415
  46.0 3.3 %collective-permute-start.7 = (bf16[2,48,256]{2,1,0:T(8,128)(2,1)S(1)}, bf16[2,48,256]{2,1,0:T(8,128)(2,1)S(1)}, u32[]{:S(2)}, u32[]{:S(2)}) collective-permute-start(bf16[2,48,256]{2,1,0:T(8,128)(2,1)S(1)} %add_convert_fusion.6), channel_id=1, source_target_pairs={{1,0},{0,1},{3,2},{2,3},{5,4},{4,5},{7,6},{6,7},{9,8},{8,9},{11,10... | collective-permute-start | bytes 147464 | tf_op jit(solution)/shard_map/ppermute | solution.py:415
  49.4 7.1 %collective-permute-start.8 = (bf16[2,48,256]{2,1,0:T(8,128)(2,1)S(1)}, bf16[2,48,256]{2,1,0:T(8,128)(2,1)S(1)}, u32[]{:S(2)}, u32[]{:S(2)}) collective-permute-start(bf16[2,48,256]{2,1,0:T(8,128)(2,1)S(1)} %add_convert_fusion.5), channel_id=1, source_target_pairs={{64,0},{65,1},{66,2},{67,3},{68,4},{69,5},{70,6},{71,7},{72,8},{73... | collective-permute-start | bytes 147464 | tf_op jit(solution)/shard_map/ppermute | solution.py:415
  56.5 4.5 %collective-permute-start.9 = (bf16[2,48,256]{2,1,0:T(8,128)(2,1)S(1)}, bf16[2,48,256]{2,1,0:T(8,128)(2,1)S(1)}, u32[]{:S(2)}, u32[]{:S(2)}) collective-permute-start(bf16[2,48,256]{2,1,0:T(8,128)(2,1)S(1)} %add_convert_fusion.4), channel_id=1, source_target_pairs={{128,0},{129,1},{130,2},{131,3},{132,4},{133,5},{134,6},{135,7},{1... | collective-permute-start | bytes 147464 | tf_op jit(solution)/shard_map/ppermute | solution.py:415
  61.1 3.0 %collective-permute-start.10 = (bf16[2,48,256]{2,1,0:T(8,128)(2,1)S(1)}, bf16[2,48,256]{2,1,0:T(8,128)(2,1)S(1)}, u32[]{:S(2)}, u32[]{:S(2)}) collective-permute-start(bf16[2,48,256]{2,1,0:T(8,128)(2,1)S(1)} %add_convert_fusion.3), channel_id=1, source_target_pairs={{2,0},{3,1},{0,2},{1,3},{6,4},{7,5},{4,6},{5,7},{10,8},{11,9},{8,1... | collective-permute-start | bytes 147464 | tf_op jit(solution)/shard_map/ppermute | solution.py:415
  61.2 19.0 %collective-permute-start.12 = (bf16[2,108,1024]{2,1,0:T(8,128)(2,1)S(1)}, bf16[2,108,1024]{2,1,0:T(8,128)(2,1)S(1)}, u32[]{:S(2)}, u32[]{:S(2)}) collective-permute-start(bf16[2,108,1024]{2,1,0:T(8,128)(2,1)S(1)} %get-tuple-element.166), channel_id=1, source_target_pairs={{15,0},{0,1},{1,2},{2,3},{3,4},{4,5},{5,6},{6,7},{7,8},{8,9},{9,10... | collective-permute-start | bytes 1327112 | tf_op jit(solution)/shard_map/ppermute | solution.py:398
  64.1 7.6 %collective-permute-start.11 = (bf16[2,48,256]{2,1,0:T(8,128)(2,1)S(1)}, bf16[2,48,256]{2,1,0:T(8,128)(2,1)S(1)}, u32[]{:S(2)}, u32[]{:S(2)}) collective-permute-start(bf16[2,48,256]{2,1,0:T(8,128)(2,1)S(1)} %add_convert_fusion.2), channel_id=1, source_target_pairs={{4,0},{5,1},{6,2},{7,3},{0,4},{1,5},{2,6},{3,7},{12,8},{13,9},{14,... | collective-permute-start | bytes 147464 | tf_op jit(solution)/shard_map/ppermute | solution.py:415
  66.4 13.8 %collective-permute-start.13 = (bf16[2,36,1024]{2,1,0:T(8,128)(2,1)S(1)}, bf16[2,36,1024]{2,1,0:T(8,128)(2,1)S(1)}, u32[]{:S(2)}, u32[]{:S(2)}) collective-permute-start(bf16[2,36,1024]{2,1,0:T(8,128)(2,1)S(1)} %get-tuple-element.167), channel_id=1, source_target_pairs={{255,0},{240,1},{241,2},{242,3},{243,4},{244,5},{245,6},{246,7},{2... | collective-permute-start | bytes 442376 | tf_op jit(solution)/shard_map/ppermute | solution.py:398
  71.6 8.6 %collective-permute-start.14 = (bf16[2,36,1024]{2,1,0:T(8,128)(2,1)S(1)}, bf16[2,36,1024]{2,1,0:T(8,128)(2,1)}, u32[]{:S(2)}, u32[]{:S(2)}) collective-permute-start(bf16[2,36,1024]{2,1,0:T(8,128)(2,1)S(1)} %get-tuple-element.168), channel_id=1, source_target_pairs={{240,0},{241,1},{242,2},{243,3},{244,4},{245,5},{246,6},{247,7},{2... | collective-permute-start | bytes 442376 | tf_op jit(solution)/shard_map/ppermute | solution.py:398
  81.6 6.9 %collective-permute-start.15 = (bf16[2,48,256]{2,1,0:T(8,128)(2,1)S(1)}, bf16[2,48,256]{2,1,0:T(8,128)(2,1)S(1)}, u32[]{:S(2)}, u32[]{:S(2)}) collective-permute-start(bf16[2,48,256]{2,1,0:T(8,128)(2,1)S(1)} %add_convert_fusion.1), channel_id=1, source_target_pairs={{8,0},{9,1},{10,2},{11,3},{12,4},{13,5},{14,6},{15,7},{0,8},{1,9},... | collective-permute-start | bytes 147464 | tf_op jit(solution)/shard_map/ppermute | solution.py:415
  88.5 4.4 %collective-permute-start.16 = (bf16[2,48,256]{2,1,0:T(8,128)(2,1)S(1)}, bf16[2,48,256]{2,1,0:T(8,128)(2,1)S(1)}, u32[]{:S(2)}, u32[]{:S(2)}) collective-permute-start(bf16[2,48,256]{2,1,0:T(8,128)(2,1)S(1)} %add_convert_fusion.mine_ref), channel_id=1, source_target_pairs={{16,0},{17,1},{18,2},{19,3},{20,4},{21,5},{22,6},{23,7},{24,8},{25... | collective-permute-start | bytes 147464 | tf_op jit(solution)/shard_map/ppermute | solution.py:415
where the time goes:
time: 93.9 us; the launch traced here: 93.7 us
  starting transfers between devices  40.2 us (43%)
  Pallas kernels  29.6 us (32%)
  waiting for transfers between devices  17.4 us (19%)
  other arithmetic  4.02 us (4%)
  local copies, waits for them, and re-layouts  1.56 us (2%)
  between operations  0.95 us (1%)
    ppermute x8, starting transfers between devices, shifted(): return lax.ppermute(block, ('lon', 'lat'), route)  26.9 us
    pallas_call x6, Pallas kernels, call(): pl.pallas_call(kernel, in_specs=[SMEM_SPEC] * len(scalars) + [VMEM_SPEC]...  24.6 us
    ppermute x9, starting transfers between devices, partner(): return lax.ppermute(block, ('lon', 'lat'), route)  13.2 us
    ppermute x8, waiting for transfers between devices, shifted(): return lax.ppermute(block, ('lon', 'lat'), route)  10.6 us
    ppermute x9, waiting for transfers between devices, partner(): return lax.ppermute(block, ('lon', 'lat'), route)  6.86 us
    convert_element_type x2, other arithmetic, add_back(): return (field.astype(F32) + back.astype(F32)).astype(BF16)  3.88 us
    pallas_call x1, Pallas kernels, run_stage(): pl.pallas_call(stage_kernel, in_specs=[pl.BlockSpec(memory_space=pltpu.HB...  3.48 us
  transfers between devices with their start and end apart: 17, of which 7 were waited for; matrix products, arithmetic and copies ran while one was open for 4% of the time, Pallas kernels for 21%

commit v1 on v0

--- a/solution.py
+++ b/solution.py
@@ -101,29 +101,37 @@
     return slice(i * D + g * GW, i * D + (g + 1) * GW)
 
 
-def pack_kernel(*refs):
-    sources, outs, fields, sems = refs[:3], refs[3:8], refs[8:11], refs[11]
-    copies = [pltpu.make_async_copy(a, b, sems.at[i]) for i, (a, b) in enumerate(zip(sources, fields))]
+def copy_in(pairs, sems):
+    copies = [pltpu.make_async_copy(a, b, sems.at[i]) for i, (a, b) in enumerate(pairs)]
     for copy in copies:
         copy.start()
     for copy in copies:
         copy.wait()
-    *belows, corner, side = outs
-    for i, field in enumerate(fields):
-        below = belows[i].at[0]
-        below[:72] = field[:6, 3:9].reshape(72, D)
-        below[72:] = field[:6, 9:].reshape(36, D)
-        corner[i] = field[:6, :3].reshape(36, D)
-        side[i] = field[6:, :3].reshape(36, D)
+
+
+def cut_below(rows, out):
+    out[:72] = rows[:, :6].reshape(72, D)
+    out[72:] = rows[:, 6:].reshape(36, D)
+
+
+def pack_kernel(x_b, cot, x_a, below, corner, side, upper, *rest):
+    firsts, sems = rest[:3], rest[3]
+    pairs = [(a.at[:, :3], b) for a, b in zip((x_b, cot, x_a), firsts)]
+    copy_in([(x_b.at[:6, 3:], upper), *pairs], sems)
+    cut_below(upper, below.at[0])
+    for i, first in enumerate(firsts):
+        corner[i] = first[:6].reshape(36, D)
+        side[i] = first[6:].reshape(36, D)
+
+
+def pack_rest_kernel(cot, x_a, below, first, second, sems):
+    copy_in([(cot.at[:6, 3:], first), (x_a.at[:6, 3:], second)], sems)
+    cut_below(first, below.at[0])
+    cut_below(second, below.at[1])
 
 
 def stage_kernel(*refs):
-    sources, outs, sems = refs[:2], refs[2:4], refs[4]
-    copies = [pltpu.make_async_copy(a, b, sems.at[i]) for i, (a, b) in enumerate(zip(sources, outs))]
-    for copy in copies:
-        copy.start()
-    for copy in copies:
-        copy.wait()
+    copy_in(zip(refs[:2], refs[2:4]), refs[4])
 
 
 def pieces_of(field, below, corner, side):
@@ -148,7 +156,7 @@
     polar_ref, field, below, corner, side, gain_ref, wqkv_ref, pd_ref, pu_ref,
     normed_ref, low_ref, context_ref, x_ref, bias_ref,
 ):
-    assemble(pieces_of(field, below.at[0], corner.at[2], side.at[2]), x_ref)
+    assemble(pieces_of(field, below.at[1], corner.at[2], side.at[2]), x_ref)
     standard, _ = layer_norm(x_ref[...])
     normed = (standard * gain_ref[...]).astype(BF16)
     normed_ref[...] = normed
@@ -260,6 +268,22 @@
     take_apart(rows_ref, (o0, o1, o2, o3, o4))
 
 
+def add_kernel(field_a, field_b, own0_a, own1_a, own0_b, own1_b, below, corner, side, out_a, out_b):
+    parts = ((field_a, own0_a.at[0], own1_a.at[0], out_a), (field_b, own0_b, own1_b, out_b))
+    for i, (field, own0, own1, out) in enumerate(parts):
+        places = (
+            (slice(0, 6), slice(0, 3), corner[i]),
+            (slice(0, 6), slice(3, 9), below[i, :72]),
+            (slice(0, 6), slice(9, 12), below[i, 72:]),
+            (slice(6, 12), slice(0, 3), side[i]),
+            (slice(6, 12), slice(3, 9), own0[...]),
+            (slice(6, 12), slice(9, 12), own1[...]),
+        )
+        for rows, cols, piece in places:
+            here = field[rows, cols]
+            out[rows, cols] = (here.astype(F32) + piece.reshape(here.shape).astype(F32)).astype(BF16)
+
+
 def clip_kernel(first_ref, mine_ref, other_ref, qd_ref, qu_ref, od_ref, ou_ref):
     mine, other = mine_ref[...].astype(F32), other_ref[...].astype(F32)
     total = jnp.sum(jnp.sum(mine * mine, axis=(0, 1)) + jnp.sum(other * other, axis=(0, 1)))
@@ -305,37 +329,34 @@
 BIAS_SCRATCH = pltpu.VMEM((WIN, GQ), F32)
 
 
-def run_pack(x_b, cot, x_a):
-    fields = [pltpu.with_memory_space_constraint(a, pltpu.HBM) for a in (x_b, cot, x_a)]
+def call_far(kernel, name, us, arrays, outs, buffers, copies):
     return pl.pallas_call(
-        pack_kernel,
-        in_specs=[pl.BlockSpec(memory_space=pltpu.HBM)] * 3,
-        out_specs=[VMEM_SPEC] * 5,
-        out_shape=[
-            jax.ShapeDtypeStruct(shape, BF16)
-            for shape in ((1, 108, D), (1, 108, D), (1, 108, D), (3, 36, D), (3, 36, D))
-        ],
+        kernel,
+        in_specs=[pl.BlockSpec(memory_space=pltpu.HBM)] * len(arrays),
+        out_specs=[VMEM_SPEC] * len(outs),
+        out_shape=[jax.ShapeDtypeStruct(shape, BF16) for shape in outs],
         scratch_shapes=[
-            *[pltpu.VMEM((12, 12, 2, D), BF16) for _ in range(3)],
-            pltpu.SemaphoreType.DMA((3,)),
+            *[pltpu.VMEM(shape, BF16) for shape in buffers],
+            pltpu.SemaphoreType.DMA((copies,)),
         ],
         compiler_params=pltpu.CompilerParams(vmem_limit_bytes=VMEM),
-        cost_estimate=cost(20),
-        name="pack",
-    )(*fields)
+        cost_estimate=cost(us),
+        name=name,
+    )(*[pltpu.with_memory_space_constraint(a, pltpu.HBM) for a in arrays])
+
+
+def run_pack(x_b, cot, x_a):
+    outs = [(1, 108, D), (3, 36, D), (3, 36, D)]
+    buffers = [(6, 9, 2, D)] + [(12, 3, 2, D)] * 3
+    return call_far(pack_kernel, "pack", 20, [x_b, cot, x_a], outs, buffers, 4)
+
+
+def run_pack_rest(cot, x_a):
+    return call_far(pack_rest_kernel, "pack_rest", 2, [cot, x_a], [(2, 108, D)], [(6, 9, 2, D)] * 2, 2)[0]
 
 
 def run_stage(wqkv, wo):
-    return pl.pallas_call(
-        stage_kernel,
-        in_specs=[pl.BlockSpec(memory_space=pltpu.HBM)] * 2,
-        out_specs=[VMEM_SPEC] * 2,
-        out_shape=[jax.ShapeDtypeStruct(a.shape, BF16) for a in (wqkv, wo)],
-        scratch_shapes=[pltpu.SemaphoreType.DMA((2,))],
-        compiler_params=pltpu.CompilerParams(vmem_limit_bytes=VMEM),
-        cost_estimate=cost(3),
-        name="stage",
-    )(*[pltpu.with_memory_space_constraint(a, pltpu.HBM) for a in (wqkv, wo)])
+    return call_far(stage_kernel, "stage", 3, [wqkv, wo], [wqkv.shape, wo.shape], [], 2)
 
 
 def run_forward_first(polar, field, halo, weights):
@@ -383,6 +404,10 @@
     )
 
 
+def run_add(*arrays):
+    return call(add_kernel, "add", 3, [], arrays, [((12, 12, 2, D), BF16)] * 2, [])
+
+
 def run_clip(first, mine, other):
     outs = [((RANK, n), F32) for n in (D, 3 * D, D, D)]
     return call(clip_kernel, "clip", 1, [first], [mine, other], outs, [])
@@ -398,15 +423,6 @@
     return lax.ppermute(block, ("lon", "lat"), route)
 
 
-def add_back(field, own0, below, corner, own1, side):
-    grid6 = lambda a: a.reshape(6, 6, 2, D)
-    grid3 = lambda a: a.reshape(6, 3, 2, D)
-    upper = jnp.concatenate([grid3(corner), grid6(below[:72]), grid3(below[72:])], axis=1)
-    lower = jnp.concatenate([grid3(side), grid6(own0), grid3(own1)], axis=1)
-    back = jnp.transpose(jnp.concatenate([upper, lower], axis=0), (2, 0, 1, 3))
-    return (field.astype(F32) + back.astype(F32)).astype(BF16)
-
-
 def partner(block, lon_bit, lat_bit):
     n_lon, n_lat = lax.axis_size("lon"), lax.axis_size("lat")
     route = [
@@ -415,14 +431,18 @@
     return lax.ppermute(block, ("lon", "lat"), route)
 
 
-def exchange(total, pair, work=None, args=()):
+def exchange(total, pairs, work=None, args=()):
     sent = total.astype(BF16)
-    if work is None:
-        return sent.astype(F32) + partner(sent, *pair).astype(F32), None
-    sent, args = lax.optimization_barrier((sent, args))
-    got = partner(sent, *pair)
-    got, done = lax.optimization_barrier((got, work(*args)))
-    return sent.astype(F32) + got.astype(F32), done
+    done = None
+    if work is not None:
+        sent, args = lax.optimization_barrier((sent, args))
+    got = [partner(sent, *pair) for pair in pairs]
+    if work is not None:
+        got, done = lax.optimization_barrier((got, work(*args)))
+    total = sent.astype(F32)
+    for other in got:
+        total = total + other.astype(F32)
+    return total, done
 
 
 def per_device(input_a, input_b, cot_b, gain, wqkv, wo, pd, pu, od, ou):
@@ -430,21 +450,19 @@
     polar = (lax.axis_index("lat") == n_lat - 1).astype(jnp.int32).reshape(1)
 
     x_b, cot, x_a = (jnp.transpose(field, (1, 2, 0, 3)) for field in (input_b, cot_b, input_a))
-    below_x, below_cot, below_a, corner, side = run_pack(x_b, cot, x_a)
-    wqkv, wo, below_x = lax.optimization_barrier((wqkv, wo, below_x))
-    staged = run_stage(wqkv, wo)
+    below_x, corner, side = run_pack(x_b, cot, x_a)
+    below_x, cot_rest, x_a_rest = lax.optimization_barrier((below_x, cot, x_a))
     below_x = shifted(below_x, 0, 1)
     corner = shifted(corner, 1, 1)
     side = shifted(side, 1, 0)
-    wqkv, wo, below_x, corner, side, below_cot = lax.optimization_barrier(
-        (*staged, below_x, corner, side, below_cot)
-    )
+    below_rest = run_pack_rest(cot_rest, x_a_rest)
+    below_rest, wqkv, wo = lax.optimization_barrier((below_rest, wqkv, wo))
+    below_rest = shifted(below_rest, 0, 1)
+    wqkv, wo = run_stage(wqkv, wo)
     weights = (gain.reshape(1, D), wqkv, wo, pd.T, pu, od.T, ou)
     rows_b, *saved = run_encode(polar, x_b, (below_x, corner, side), weights)
-    below_cot = shifted(below_cot, 0, 1)
-    saved, below_cot, below_a = lax.optimization_barrier((saved, below_cot, below_a))
-    gp, clq, grads = run_grads(cot, (below_cot, corner, side), saved, weights)
-    below_a = shifted(below_a, 0, 1)
+    halo = (below_rest, corner, side)
+    gp, clq, grads = run_grads(cot, halo, saved, weights)
 
     core = lax.rem(lax.axis_index("lon"), 2)
     halves = grads[:2], grads[2:]
@@ -452,39 +470,35 @@
     sent = jnp.where(core == 0, halves[1], halves[0]).astype(BF16)
     total = kept + partner(sent, 1, 0).astype(F32)
 
-    pairs = [(2, 0), (0, 1), (4, 0), (8, 0), (0, 2), (0, 4), (0, 8)]
-    pairs = [(a, b) for a, b in pairs if a < n_lon and b < n_lat]
+    steps = [[(0, 8)], [(0, 1)], [(8, 0)], [(0, 2)], [(0, 4)], [(2, 0)], [(4, 0)]]
+    steps = [step for step in steps if all(a < n_lon and b < n_lat for a, b in step)]
     total, (own0_b, below_b, corner_b, own1_b, side_b) = exchange(
-        total, pairs[0], lambda *a: run_input_grad(*a, weights), (rows_b, gp, clq)
+        total, steps[0], lambda *a: run_input_grad(*a, weights), (rows_b, gp, clq)
     )
     total, saved = exchange(
         total,
-        pairs[1],
+        steps[1],
         lambda *halo: run_forward_first(polar, x_a, halo, weights),
-        (below_a, corner, side),
+        halo,
     )
     total, (own0_a, below, corner, own1_a, side) = exchange(
         total,
-        pairs[2],
+        steps[2],
         lambda *a: run_forward_second(polar, a[:3], a[3:], weights),
         (*saved, below_b, corner_b, side_b),
     )
     below = shifted(below, 0, -1)
     corner = shifted(corner, -1, -1)
     side = shifted(side, -1, 0)
-    for pair in pairs[3:-1]:
-        total = exchange(total, pair)[0]
-    total, (output_a, input_grad_b) = exchange(
-        total,
-        pairs[-1],
-        lambda below, corner, side: (
-            add_back(input_a, own0_a, below[0], corner[0], own1_a, side[0]),
-            add_back(cot_b, own0_b, below[1], corner[1], own1_b, side[1]),
-        ),
-        (below, corner, side),
-    )
-    total = total.astype(BF16)
-    qd, qu, od_grad, ou_grad = run_clip(core.reshape(1), total, partner(total, 1, 0))
+    for step in steps[3:-1]:
+        total = exchange(total, step)[0]
+    sent = total.astype(BF16)
+    outs = run_add(x_a, cot, own0_a, own1_a, own0_b, own1_b, below, corner, side)
+    got, output_a, input_grad_b = lax.optimization_barrier((partner(sent, *steps[-1][0]), *outs))
+    total = (sent.astype(F32) + got.astype(F32)).astype(BF16)
+    other = partner(total, 1, 0)
+    output_a, input_grad_b = (jnp.transpose(a, (2, 0, 1, 3)) for a in (output_a, input_grad_b))
+    qd, qu, od_grad, ou_grad = run_clip(core.reshape(1), total, other)
     return output_a, input_grad_b, qd.T, qu, od_grad.T, ou_grad
 
 

time: 93.9 us -> 89 us (0.948)
  other arithmetic: 4.02 us -> 0.14 us
  Pallas kernels: 29.6 us -> 32.5 us
  starting transfers between devices: 40.2 us -> 38 us
  local copies, waits for them, and re-layouts: 1.56 us -> 0.04 us
    ppermute x8 -> x7, waiting for transfers between devices: 10.6 us -> 3.96 us  [shifted(): return lax.ppermute(block, ('lon', 'lat'), route)]
    ppermute x9, waiting for transfers between devices: 6.86 us -> 13.3 us  [partner(): return lax.ppermute(block, ('lon', 'lat'), route)]
    ppermute x8 -> x7, starting transfers between devices: 26.9 us -> 22.3 us  [shifted(): return lax.ppermute(block, ('lon', 'lat'), route)]
    convert_element_type x3 -> x2, other arithmetic: 3.89 us -> 0.03 us  [the longest x1 0.01 us: per_device(): sent = total.astype(BF16)]
    ppermute x9, starting transfers between devices: 13.2 us -> 15.7 us  [partner(): return lax.ppermute(block, ('lon', 'lat'), route)]
    pallas_call x6 -> x7, Pallas kernels: 24.6 us -> 26.6 us  [call(): pl.pallas_call(kernel, in_specs=[SMEM_SPEC] * len(scalars) + [VMEM_SPEC]...]
    slice x3 -> x0, local copies, waits for them, and re-layouts: 0.98 us -> none  [the longest x1 0.94 us: per_device(): side[1]]
    pallas_call x2 -> x3, Pallas kernels: 5.06 us -> 5.87 us  [call_far(): pl.pallas_call(kernel, in_specs=[pl.BlockSpec(memory_space=pltpu.HBM)] *...]
  transfers between devices with their start and end apart: 17 -> 16, of which waited for: 7 -> 8; matrix products, arithmetic and copies ran while one was open for 4% -> 0% of each run, Pallas kernels for 21% -> 26%
where the time goes in v1:
time: 89 us; the launch traced here: 88.9 us
  starting transfers between devices  38 us (43%)
  Pallas kernels  32.5 us (37%)
  waiting for transfers between devices  17.3 us (19%)
  between operations  0.9 us (1%)
    pallas_call x7, Pallas kernels, call(): pl.pallas_call(kernel, in_specs=[SMEM_SPEC] * len(scalars) + [VMEM_SPEC]...  26.6 us
    ppermute x7, starting transfers between devices, shifted(): return lax.ppermute(block, ('lon', 'lat'), route)  22.3 us
    ppermute x9, starting transfers between devices, partner(): return lax.ppermute(block, ('lon', 'lat'), route)  15.7 us
    ppermute x9, waiting for transfers between devices, partner(): return lax.ppermute(block, ('lon', 'lat'), route)  13.3 us
    pallas_call x3, Pallas kernels, call_far(): pl.pallas_call(kernel, in_specs=[pl.BlockSpec(memory_space=pltpu.HBM)] *...  5.87 us
    ppermute x7, waiting for transfers between devices, shifted(): return lax.ppermute(block, ('lon', 'lat'), route)  3.96 us
  transfers between devices with their start and end apart: 16, of which 8 were waited for; matrix products, arithmetic and copies ran while one was open for 0% of the time, Pallas kernels for 26%

profile of v1, /device:TPU:1, one launch (start us, length us, event | category | flops | bytes accessed | tf_op | source)
XLA Modules:
  0.0 88.9 jit_solution(2695835633598884911)
XLA Ops:
  0.6 1.3 %pack.1 = (bf16[1,108,1024]{2,1,0:T(8,128)(2,1)S(1)}, bf16[3,36,1024]{2,1,0:T(8,128)(2,1)S(1)}, bf16[3,36,1024]{2,1,0:T(8,128)(2,1)S(1)}) custom-call(bf16[12,12,2,1024]{3,2,1,0:T(2,128)(2,1)} %bitcast.12, bf16[12,12,2,1024]{3,2,1,0:T(2,128)(2,1)} %bitcast.18, bf16[12,12,2,1024]{3,2,1,0:T(2,128)(2,1)} %bitcast.14), custom_call_target="tpu_custom_call" | custom-call | flops 20000000000 | bytes 4000000 | tf_op jit(solution)/shard_map/pack/pallas_call | solution.py:333
  1.9 7.4 %collective-permute-start.3 = (bf16[1,108,1024]{2,1,0:T(8,128)(2,1)S(1)}, bf16[1,108,1024]{2,1,0:T(8,128)(2,1)S(1)}, u32[]{:S(2)}, u32[]{:S(2)}) collective-permute-start(bf16[1,108,1024]{2,1,0:T(8,128)(2,1)S(1)} %get-tuple-element.86), channel_id=1, source_target_pairs={{1,0},{2,1},{3,2},{4,3},{5,4},{6,5},{7,6},{8,7},{9,8},{10,9},{11,1... | collective-permute-start | bytes 663560 | tf_op jit(solution)/shard_map/ppermute | solution.py:423
  9.3 1.1 %collective-permute-start.1 = (bf16[3,36,1024]{2,1,0:T(8,128)(2,1)S(1)}, bf16[3,36,1024]{2,1,0:T(8,128)(2,1)S(1)}, u32[]{:S(2)}, u32[]{:S(2)}) collective-permute-start(bf16[3,36,1024]{2,1,0:T(8,128)(2,1)S(1)} %get-tuple-element.84), channel_id=1, source_target_pairs={{17,0},{18,1},{19,2},{20,3},{21,4},{22,5},{23,6},{24,7},{25,8},{26... | collective-permute-start | bytes 663560 | tf_op jit(solution)/shard_map/ppermute | solution.py:423
  10.4 3.6 %collective-permute-start.2 = (bf16[3,36,1024]{2,1,0:T(8,128)(2,1)S(1)}, bf16[3,36,1024]{2,1,0:T(8,128)(2,1)S(1)}, u32[]{:S(2)}, u32[]{:S(2)}) collective-permute-start(bf16[3,36,1024]{2,1,0:T(8,128)(2,1)S(1)} %get-tuple-element.85), channel_id=1, source_target_pairs={{16,0},{17,1},{18,2},{19,3},{20,4},{21,5},{22,6},{23,7},{24,8},{25... | collective-permute-start | bytes 663560 | tf_op jit(solution)/shard_map/ppermute | solution.py:423
  14.0 1.1 %pack_rest.1 = bf16[2,108,1024]{2,1,0:T(8,128)(2,1)S(1)} custom-call(bf16[12,12,2,1024]{3,2,1,0:T(2,128)(2,1)} %bitcast.19, bf16[12,12,2,1024]{3,2,1,0:T(2,128)(2,1)} %bitcast.15), custom_call_target="tpu_custom_call" | custom-call | flops 2000000000 | bytes 4000000 | tf_op jit(solution)/shard_map/pack_rest/pallas_call | solution.py:333
  15.1 1.0 %collective-permute-start = (bf16[2,108,1024]{2,1,0:T(8,128)(2,1)S(1)}, bf16[2,108,1024]{2,1,0:T(8,128)(2,1)S(1)}, u32[]{:S(2)}, u32[]{:S(2)}) collective-permute-start(bf16[2,108,1024]{2,1,0:T(8,128)(2,1)S(1)} %pack_rest.1), channel_id=1, source_target_pairs={{1,0},{2,1},{3,2},{4,3},{5,4},{6,5},{7,6},{8,7},{9,8},{10,9},{11,1... | collective-permute-start | bytes 1327112 | tf_op jit(solution)/shard_map/ppermute | solution.py:423
  16.1 0.0 copy-start
  16.1 0.0 copy-start.3
  16.1 0.0 copy-start.4
  16.1 0.0 copy-start.5
  16.1 0.0 copy-start.7
  16.1 3.5 %stage.1 = (bf16[1024,3072]{1,0:T(8,128)(2,1)S(1)}, bf16[1024,1024]{1,0:T(8,128)(2,1)S(1)}) custom-call(bf16[1024,3072]{1,0:T(8,128)(2,1)} %refs_0_, bf16[1024,1024]{1,0:T(8,128)(2,1)} %refs_1_), custom_call_target="tpu_custom_call" | custom-call | flops 3000000000 | bytes 4000000 | tf_op jit(solution)/shard_map/stage/pallas_call | solution.py:333
  19.6 0.0 collective-permute-done.3.below
  19.6 0.0 collective-permute-done.1.corner
  19.7 0.0 collective-permute-done.2.side
  19.7 0.0 copy-done
  19.7 0.0 copy-done.3
  19.7 0.0 copy-done.4
  19.7 0.0 copy-done.5
  19.7 0.0 copy-done.7
  19.7 0.0 copy-start.2
  19.7 0.0 copy-start.6
  19.7 6.5 %encode.1 = (f32[288,1024]{1,0:T(8,128)S(1)}, bf16[288,1024]{1,0:T(8,128)(2,1)S(1)}, bf16[8,288]{1,0:T(8,128)(2,1)S(1)}, bf16[288,3072]{1,0:T(8,128)(2,1)S(1)}, ...) custom-call(s32[1]{0:T(128)} %bitcast.3.polar_ref, ...), custom_call_target="tpu_custom_call" | custom-call | flops 7000000000 | bytes 4000000 | tf_op jit(solution)/shard_map/encode/pallas_call | solution.py:315
  26.2 2.5 %collective-permute-done.below = bf16[2,108,1024]{2,1,0:T(8,128)(2,1)S(1)} collective-permute-done((bf16[2,108,1024]{2,1,0:T(8,128)(2,1)S(1)}, bf16[2,108,1024]{2,1,0:T(8,128)(2,1)S(1)}, u32[]{:S(2)}, u32[]{:S(2)}) %collective-permute-start) | collective-permute-done | bytes 442400 | tf_op jit(solution)/shard_map/ppermute | solution.py:423
  28.7 0.0 copy-done.2
  28.7 0.0 copy-done.6
  28.7 7.1 %grads.1 = (bf16[288,3072]{1,0:T(8,128)(2,1)S(1)}, bf16[288,8]{1,0:T(8,128)(2,1)S(1)}, f32[4,48,256]{2,1,0:T(8,128)S(1)}) custom-call(bf16[12,12,2,1024]{3,2,1,0:T(2,128)(2,1)S(1)} %bitcast.20, bf16[2,108,1024]{2,1,0:T(8,128)(2,1)S(1)} %collective-permute-done.below, bf16[3,36,1024]{2,1,0:T(8,128)(2,1)S(1)} %collective-permute-done.1.corner, ...), custom_call_target="tpu_custom_call" | custom-call | flops 7000000000 | bytes 4000000 | tf_op jit(solution)/shard_map/grads/pallas_call | solution.py:315
  35.9 7.5 %collective-permute-start.4 = (bf16[2,48,256]{2,1,0:T(8,128)(2,1)S(1)}, bf16[2,48,256]{2,1,0:T(8,128)(2,1)S(1)}, u32[]{:S(2)}, u32[]{:S(2)}) collective-permute-start(bf16[2,48,256]{2,1,0:T(8,128)(2,1)S(1)} %select_convert_fusion), channel_id=1, source_target_pairs={{16,0},{17,1},{18,2},{19,3},{20,4},{21,5},{22,6},{23,7},{24,8},{25... | collective-permute-start | bytes 147464 | tf_op jit(solution)/shard_map/ppermute | solution.py:431
  43.4 0.9 collective-permute-done.4
  44.3 0.0 copy-start.1
  44.3 0.3 collective-permute-start.5
  44.6 2.5 %input_grad.1 = (bf16[72,1024]{1,0:T(8,128)(2,1)S(1)}, bf16[108,1024]{1,0:T(8,128)(2,1)S(1)}, bf16[36,1024]{1,0:T(8,128)(2,1)S(1)}, bf16[36,1024]{1,0:T(8,128)(2,1)S(1)}, bf16[36,1024]{1,0:T(8,128)(2,1)S(1)}) custom-call(f32[288,1024]{1,0:T(8,128)S(1)} %get-tuple-element.102.x_ref, f32[1,1024]{1,0:T(1,128)S(1)} %bitcast.29, ...), custom_call_target="tpu_custom_call" | custom-call | flops 3000000000 | bytes 4000000 | tf_op jit(solution)/shard_map/input_grad/pallas_call | solution.py:315
  47.1 4.4 %collective-permute-done.5 = bf16[2,48,256]{2,1,0:T(8,128)(2,1)S(1)} collective-permute-done((bf16[2,48,256]{2,1,0:T(8,128)(2,1)S(1)}, bf16[2,48,256]{2,1,0:T(8,128)(2,1)S(1)}, u32[]{:S(2)}, u32[]{:S(2)}) %collective-permute-start.5) | collective-permute-done | bytes 49184 | tf_op jit(solution)/shard_map/ppermute | solution.py:431
  51.5 0.1 collective-permute-start.6
  51.6 0.0 copy-done.1
  51.6 3.3 %forward_first.1 = (bf16[288,1024]{1,0:T(8,128)(2,1)S(1)}, bf16[288,8]{1,0:T(8,128)(2,1)S(1)}, bf16[288,512]{1,0:T(8,128)(2,1)S(1)}) custom-call(s32[1]{0:T(128)} %bitcast.3.polar_ref, bf16[12,12,2,1024]{3,2,1,0:T(2,128)(2,1)S(1)} %bitcast.16, bf16[2,108,1024]{2,1,0:T(8,128)(2,1)S(1)} %collective-permute-done.below, ...), custom_call_target="tpu_custom_call" | custom-call | flops 4000000000 | bytes 4000000 | tf_op jit(solution)/shard_map/forward_first/pallas_call | solution.py:315
  54.9 0.0 collective-permute-done.6
  54.9 0.4 collective-permute-start.7
  55.3 4.4 %forward_second.1 = (bf16[1,72,1024]{2,1,0:T(8,128)(2,1)S(1)}, bf16[2,108,1024]{2,1,0:T(8,128)(2,1)S(1)}, bf16[2,36,1024]{2,1,0:T(8,128)(2,1)S(1)}, bf16[1,36,10...) custom-call(s32[1]{0:T(128)} %bitcast.3.polar_ref, bf16[288,1024]{1,0:T(8,128)(2,1)S(1)} %get-tuple-element.126.normed_ref, ...), custom_call_target="tpu_custom_call" | custom-call | flops 4000000000 | bytes 4000000 | tf_op jit(solution)/shard_map/forward_second/pallas_call | solution.py:315
  59.7 0.0 collective-permute-done.7
  59.7 0.1 collective-permute-start.8
  59.8 2.9 %collective-permute-done.8 = bf16[2,48,256]{2,1,0:T(8,128)(2,1)S(1)} collective-permute-done((bf16[2,48,256]{2,1,0:T(8,128)(2,1)S(1)}, bf16[2,48,256]{2,1,0:T(8,128)(2,1)S(1)}, u32[]{:S(2)}, u32[]{:S(2)}) %collective-permute-start.8) | collective-permute-done | bytes 49184 | tf_op jit(solution)/shard_map/ppermute | solution.py:431
  62.8 0.1 collective-permute-start.9
  62.9 1.2 %collective-permute-start.12 = (bf16[2,108,1024]{2,1,0:T(8,128)(2,1)S(1)}, bf16[2,108,1024]{2,1,0:T(8,128)(2,1)S(1)}, u32[]{:S(2)}, u32[]{:S(2)}) collective-permute-start(bf16[2,108,1024]{2,1,0:T(8,128)(2,1)S(1)} %get-tuple-element.142), channel_id=1, source_target_pairs={{15,0},{0,1},{1,2},{2,3},{3,4},{4,5},{5,6},{6,7},{7,8},{8,9},{9,10... | collective-permute-start | bytes 1327112 | tf_op jit(solution)/shard_map/ppermute | solution.py:423
  64.1 2.8 %collective-permute-done.9 = bf16[2,48,256]{2,1,0:T(8,128)(2,1)S(1)} collective-permute-done((bf16[2,48,256]{2,1,0:T(8,128)(2,1)S(1)}, bf16[2,48,256]{2,1,0:T(8,128)(2,1)S(1)}, u32[]{:S(2)}, u32[]{:S(2)}) %collective-permute-start.9) | collective-permute-done | bytes 49184 | tf_op jit(solution)/shard_map/ppermute | solution.py:431
  67.0 0.1 collective-permute-start.10
  67.1 8.0 %collective-permute-start.13 = (bf16[2,36,1024]{2,1,0:T(8,128)(2,1)S(1)}, bf16[2,36,1024]{2,1,0:T(8,128)(2,1)S(1)}, u32[]{:S(2)}, u32[]{:S(2)}) collective-permute-start(bf16[2,36,1024]{2,1,0:T(8,128)(2,1)S(1)} %get-tuple-element.143), channel_id=1, source_target_pairs={{255,0},{240,1},{241,2},{242,3},{243,4},{244,5},{245,6},{246,7},{2... | collective-permute-start | bytes 442376 | tf_op jit(solution)/shard_map/ppermute | solution.py:423
  75.0 0.0 collective-permute-start.14
  75.1 0.0 collective-permute-done.10
  75.1 3.5 %collective-permute-start.11 = (bf16[2,48,256]{2,1,0:T(8,128)(2,1)S(1)}, bf16[2,48,256]{2,1,0:T(8,128)(2,1)S(1)}, u32[]{:S(2)}, u32[]{:S(2)}) collective-permute-start(bf16[2,48,256]{2,1,0:T(8,128)(2,1)S(1)} %add_convert_fusion.1), channel_id=1, source_target_pairs={{64,0},{65,1},{66,2},{67,3},{68,4},{69,5},{70,6},{71,7},{72,8},{73... | collective-permute-start | bytes 147464 | tf_op jit(solution)/shard_map/ppermute | solution.py:431
  78.5 1.5 %collective-permute-done.13.corner = bf16[2,36,1024]{2,1,0:T(8,128)(2,1)S(1)} collective-permute-done((bf16[2,36,1024]{2,1,0:T(8,128)(2,1)S(1)}, bf16[2,36,1024]{2,1,0:T(8,128)(2,1)S(1)}, u32[]{:S(2)}, u32[]{:S(2)}) %collective-permute-start.13) | collective-permute-done | bytes 147488 | tf_op jit(solution)/shard_map/ppermute | solution.py:423
  80.0 0.0 collective-permute-done.14.side
  80.0 0.0 collective-permute-done.12.below
  80.0 2.1 %add.41 = (bf16[12,12,2,1024]{3,2,1,0:T(2,128)(2,1)}, bf16[12,12,2,1024]{3,2,1,0:T(2,128)(2,1)}) custom-call(bf16[12,12,2,1024]{3,2,1,0:T(2,128)(2,1)S(1)} %bitcast.17, bf16[12,12,2,1024]{3,2,1,0:T(2,128)(2,1)S(1)} %bitcast.21, bf16[1,72,1024]{2,1,0:T(8,128)(2,1)S(1)} %get-tuple-element.138.own0_a, bf16[1,36,1024]{2,1,0:T(8,128)(2,1)S(1)} %get-tuple-element.139.own1_a, ...), custom_call_target="tpu_custom_call" | custom-call | flops 3000000000 | bytes 4000000 | tf_op jit(solution)/shard_map/add/pallas_call | solution.py:315
  82.1 1.4 %collective-permute-done.11 = bf16[2,48,256]{2,1,0:T(8,128)(2,1)S(1)} collective-permute-done((bf16[2,48,256]{2,1,0:T(8,128)(2,1)S(1)}, bf16[2,48,256]{2,1,0:T(8,128)(2,1)S(1)}, u32[]{:S(2)}, u32[]{:S(2)}) %collective-permute-start.11) | collective-permute-done | bytes 49184 | tf_op jit(solution)/shard_map/ppermute | solution.py:431
  83.5 3.7 %collective-permute-start.15 = (bf16[2,48,256]{2,1,0:T(8,128)(2,1)S(1)}, bf16[2,48,256]{2,1,0:T(8,128)(2,1)S(1)}, u32[]{:S(2)}, u32[]{:S(2)}) collective-permute-start(bf16[2,48,256]{2,1,0:T(8,128)(2,1)S(1)} %add_convert_fusion.mine_ref), channel_id=1, source_target_pairs={{16,0},{17,1},{18,2},{19,3},{20,4},{21,5},{22,6},{23,7},{24,8},{25... | collective-permute-start | bytes 147464 | tf_op jit(solution)/shard_map/ppermute | solution.py:431
  87.2 0.9 collective-permute-done.15.other_ref
  88.1 0.8 clip.1
  (9 shorter events, 0.1 us)
Async XLA Ops:
  1.9 17.7 %collective-permute-start.3 = (bf16[1,108,1024]{2,1,0:T(8,128)(2,1)S(1)}, bf16[1,108,1024]{2,1,0:T(8,128)(2,1)S(1)}, u32[]{:S(2)}, u32[]{:S(2)}) collective-permute-start(bf16[1,108,1024]{2,1,0:T(8,128)(2,1)S(1)} %get-tuple-element.86), channel_id=1, source_target_pairs={{1,0},{2,1},{3,2},{4,3},{5,4},{6,5},{7,6},{8,7},{9,8},{10,9},{11,1... | collective-permute-start | bytes 663560 | tf_op jit(solution)/shard_map/ppermute | solution.py:423
  9.3 10.3 %collective-permute-start.1 = (bf16[3,36,1024]{2,1,0:T(8,128)(2,1)S(1)}, bf16[3,36,1024]{2,1,0:T(8,128)(2,1)S(1)}, u32[]{:S(2)}, u32[]{:S(2)}) collective-permute-start(bf16[3,36,1024]{2,1,0:T(8,128)(2,1)S(1)} %get-tuple-element.84), channel_id=1, source_target_pairs={{17,0},{18,1},{19,2},{20,3},{21,4},{22,5},{23,6},{24,7},{25,8},{26... | collective-permute-start | bytes 663560 | tf_op jit(solution)/shard_map/ppermute | solution.py:423
  10.4 9.2 %collective-permute-start.2 = (bf16[3,36,1024]{2,1,0:T(8,128)(2,1)S(1)}, bf16[3,36,1024]{2,1,0:T(8,128)(2,1)S(1)}, u32[]{:S(2)}, u32[]{:S(2)}) collective-permute-start(bf16[3,36,1024]{2,1,0:T(8,128)(2,1)S(1)} %get-tuple-element.85), channel_id=1, source_target_pairs={{16,0},{17,1},{18,2},{19,3},{20,4},{21,5},{22,6},{23,7},{24,8},{25... | collective-permute-start | bytes 663560 | tf_op jit(solution)/shard_map/ppermute | solution.py:423
  15.1 13.6 %collective-permute-start = (bf16[2,108,1024]{2,1,0:T(8,128)(2,1)S(1)}, bf16[2,108,1024]{2,1,0:T(8,128)(2,1)S(1)}, u32[]{:S(2)}, u32[]{:S(2)}) collective-permute-start(bf16[2,108,1024]{2,1,0:T(8,128)(2,1)S(1)} %pack_rest.1), channel_id=1, source_target_pairs={{1,0},{2,1},{3,2},{4,3},{5,4},{6,5},{7,6},{8,7},{9,8},{10,9},{11,1... | collective-permute-start | bytes 1327112 | tf_op jit(solution)/shard_map/ppermute | solution.py:423
  16.1 3.5 %copy-start = (bf16[2,12,12,1024]{3,0,2,1:T(2,128)(2,1)S(1)}, bf16[2,12,12,1024]{3,0,2,1:T(2,128)(2,1)}, u32[]{:S(2)}) copy-start(bf16[2,12,12,1024]{3,0,2,1:T(2,128)(2,1)} %param.11) | copy-start | bytes 1769476
  16.1 3.6 %copy-start.3 = (bf16[8,3072]{1,0:T(8,128)(2,1)S(1)}, bf16[8,3072]{1,0:T(8,128)(2,1)}, u32[]{:S(2)}) copy-start(bf16[8,3072]{1,0:T(8,128)(2,1)} %pu_ref.7) | copy-start | bytes 147460
  16.1 3.6 %copy-start.4 = (bf16[1024,8]{0,1:T(8,128)(2,1)S(1)}, bf16[1024,8]{0,1:T(8,128)(2,1)}, u32[]{:S(2)}) copy-start(bf16[1024,8]{0,1:T(8,128)(2,1)} %param.16) | copy-start | bytes 49156
  16.1 3.6 %copy-start.5 = (bf16[1024,8]{0,1:T(8,128)(2,1)S(1)}, bf16[1024,8]{0,1:T(8,128)(2,1)}, u32[]{:S(2)}) copy-start(bf16[1024,8]{0,1:T(8,128)(2,1)} %param.18) | copy-start | bytes 49156
  16.1 3.6 %copy-start.7 = (f32[1024]{0:T(1024)S(1)}, f32[1024]{0:T(1024)}, u32[]{:S(2)}) copy-start(f32[1024]{0:T(1024)} %param.13) | copy-start | bytes 12292
  19.7 9.0 %copy-start.2 = (bf16[2,12,12,1024]{3,0,2,1:T(2,128)(2,1)S(1)}, bf16[2,12,12,1024]{3,0,2,1:T(2,128)(2,1)}, u32[]{:S(2)}) copy-start(bf16[2,12,12,1024]{3,0,2,1:T(2,128)(2,1)} %param.12) | copy-start | bytes 1769476
  19.7 9.0 %copy-start.6 = (bf16[8,1024]{1,0:T(8,128)(2,1)S(1)}, bf16[8,1024]{1,0:T(8,128)(2,1)}, u32[]{:S(2)}) copy-start(bf16[8,1024]{1,0:T(8,128)(2,1)} %ou_ref.3) | copy-start | bytes 49156
  35.9 8.4 %collective-permute-start.4 = (bf16[2,48,256]{2,1,0:T(8,128)(2,1)S(1)}, bf16[2,48,256]{2,1,0:T(8,128)(2,1)S(1)}, u32[]{:S(2)}, u32[]{:S(2)}) collective-permute-start(bf16[2,48,256]{2,1,0:T(8,128)(2,1)S(1)} %select_convert_fusion), channel_id=1, source_target_pairs={{16,0},{17,1},{18,2},{19,3},{20,4},{21,5},{22,6},{23,7},{24,8},{25... | collective-permute-start | bytes 147464 | tf_op jit(solution)/shard_map/ppermute | solution.py:431
  44.3 7.3 %copy-start.1 = (bf16[2,12,12,1024]{3,0,2,1:T(2,128)(2,1)S(1)}, bf16[2,12,12,1024]{3,0,2,1:T(2,128)(2,1)}, u32[]{:S(2)}) copy-start(bf16[2,12,12,1024]{3,0,2,1:T(2,128)(2,1)} %param.10) | copy-start | bytes 1769476
  44.3 7.2 %collective-permute-start.5 = (bf16[2,48,256]{2,1,0:T(8,128)(2,1)S(1)}, bf16[2,48,256]{2,1,0:T(8,128)(2,1)S(1)}, u32[]{:S(2)}, u32[]{:S(2)}) collective-permute-start(bf16[2,48,256]{2,1,0:T(8,128)(2,1)S(1)} %add_convert_fusion.7), channel_id=1, source_target_pairs={{8,0},{9,1},{10,2},{11,3},{12,4},{13,5},{14,6},{15,7},{0,8},{1,9},... | collective-permute-start | bytes 147464 | tf_op jit(solution)/shard_map/ppermute | solution.py:431
  51.5 3.4 %collective-permute-start.6 = (bf16[2,48,256]{2,1,0:T(8,128)(2,1)S(1)}, bf16[2,48,256]{2,1,0:T(8,128)(2,1)S(1)}, u32[]{:S(2)}, u32[]{:S(2)}) collective-permute-start(bf16[2,48,256]{2,1,0:T(8,128)(2,1)S(1)} %add_convert_fusion.6), channel_id=1, source_target_pairs={{1,0},{0,1},{3,2},{2,3},{5,4},{4,5},{7,6},{6,7},{9,8},{8,9},{11,10... | collective-permute-start | bytes 147464 | tf_op jit(solution)/shard_map/ppermute | solution.py:431
  54.9 4.8 %collective-permute-start.7 = (bf16[2,48,256]{2,1,0:T(8,128)(2,1)S(1)}, bf16[2,48,256]{2,1,0:T(8,128)(2,1)S(1)}, u32[]{:S(2)}, u32[]{:S(2)}) collective-permute-start(bf16[2,48,256]{2,1,0:T(8,128)(2,1)S(1)} %add_convert_fusion.5), channel_id=1, source_target_pairs={{128,0},{129,1},{130,2},{131,3},{132,4},{133,5},{134,6},{135,7},{1... | collective-permute-start | bytes 147464 | tf_op jit(solution)/shard_map/ppermute | solution.py:431
  59.7 3.0 %collective-permute-start.8 = (bf16[2,48,256]{2,1,0:T(8,128)(2,1)S(1)}, bf16[2,48,256]{2,1,0:T(8,128)(2,1)S(1)}, u32[]{:S(2)}, u32[]{:S(2)}) collective-permute-start(bf16[2,48,256]{2,1,0:T(8,128)(2,1)S(1)} %add_convert_fusion.4), channel_id=1, source_target_pairs={{2,0},{3,1},{0,2},{1,3},{6,4},{7,5},{4,6},{5,7},{10,8},{11,9},{8,1... | collective-permute-start | bytes 147464 | tf_op jit(solution)/shard_map/ppermute | solution.py:431
  62.8 4.2 %collective-permute-start.9 = (bf16[2,48,256]{2,1,0:T(8,128)(2,1)S(1)}, bf16[2,48,256]{2,1,0:T(8,128)(2,1)S(1)}, u32[]{:S(2)}, u32[]{:S(2)}) collective-permute-start(bf16[2,48,256]{2,1,0:T(8,128)(2,1)S(1)} %add_convert_fusion.3), channel_id=1, source_target_pairs={{4,0},{5,1},{6,2},{7,3},{0,4},{1,5},{2,6},{3,7},{12,8},{13,9},{14,... | collective-permute-start | bytes 147464 | tf_op jit(solution)/shard_map/ppermute | solution.py:431
  62.9 17.1 %collective-permute-start.12 = (bf16[2,108,1024]{2,1,0:T(8,128)(2,1)S(1)}, bf16[2,108,1024]{2,1,0:T(8,128)(2,1)S(1)}, u32[]{:S(2)}, u32[]{:S(2)}) collective-permute-start(bf16[2,108,1024]{2,1,0:T(8,128)(2,1)S(1)} %get-tuple-element.142), channel_id=1, source_target_pairs={{15,0},{0,1},{1,2},{2,3},{3,4},{4,5},{5,6},{6,7},{7,8},{8,9},{9,10... | collective-permute-start | bytes 1327112 | tf_op jit(solution)/shard_map/ppermute | solution.py:423
  67.0 8.1 %collective-permute-start.10 = (bf16[2,48,256]{2,1,0:T(8,128)(2,1)S(1)}, bf16[2,48,256]{2,1,0:T(8,128)(2,1)S(1)}, u32[]{:S(2)}, u32[]{:S(2)}) collective-permute-start(bf16[2,48,256]{2,1,0:T(8,128)(2,1)S(1)} %add_convert_fusion.2), channel_id=1, source_target_pairs={{32,0},{33,1},{34,2},{35,3},{36,4},{37,5},{38,6},{39,7},{40,8},{41... | collective-permute-start | bytes 147464 | tf_op jit(solution)/shard_map/ppermute | solution.py:431
  67.1 12.9 %collective-permute-start.13 = (bf16[2,36,1024]{2,1,0:T(8,128)(2,1)S(1)}, bf16[2,36,1024]{2,1,0:T(8,128)(2,1)S(1)}, u32[]{:S(2)}, u32[]{:S(2)}) collective-permute-start(bf16[2,36,1024]{2,1,0:T(8,128)(2,1)S(1)} %get-tuple-element.143), channel_id=1, source_target_pairs={{255,0},{240,1},{241,2},{242,3},{243,4},{244,5},{245,6},{246,7},{2... | collective-permute-start | bytes 442376 | tf_op jit(solution)/shard_map/ppermute | solution.py:423
  75.0 5.0 %collective-permute-start.14 = (bf16[2,36,1024]{2,1,0:T(8,128)(2,1)S(1)}, bf16[2,36,1024]{2,1,0:T(8,128)(2,1)S(1)}, u32[]{:S(2)}, u32[]{:S(2)}) collective-permute-start(bf16[2,36,1024]{2,1,0:T(8,128)(2,1)S(1)} %get-tuple-element.144), channel_id=1, source_target_pairs={{240,0},{241,1},{242,2},{243,3},{244,4},{245,5},{246,6},{247,7},{2... | collective-permute-start | bytes 442376 | tf_op jit(solution)/shard_map/ppermute | solution.py:423
  75.1 8.4 %collective-permute-start.11 = (bf16[2,48,256]{2,1,0:T(8,128)(2,1)S(1)}, bf16[2,48,256]{2,1,0:T(8,128)(2,1)S(1)}, u32[]{:S(2)}, u32[]{:S(2)}) collective-permute-start(bf16[2,48,256]{2,1,0:T(8,128)(2,1)S(1)} %add_convert_fusion.1), channel_id=1, source_target_pairs={{64,0},{65,1},{66,2},{67,3},{68,4},{69,5},{70,6},{71,7},{72,8},{73... | collective-permute-start | bytes 147464 | tf_op jit(solution)/shard_map/ppermute | solution.py:431
  83.5 4.6 %collective-permute-start.15 = (bf16[2,48,256]{2,1,0:T(8,128)(2,1)S(1)}, bf16[2,48,256]{2,1,0:T(8,128)(2,1)S(1)}, u32[]{:S(2)}, u32[]{:S(2)}) collective-permute-start(bf16[2,48,256]{2,1,0:T(8,128)(2,1)S(1)} %add_convert_fusion.mine_ref), channel_id=1, source_target_pairs={{16,0},{17,1},{18,2},{19,3},{20,4},{21,5},{22,6},{23,7},{24,8},{25... | collective-permute-start | bytes 147464 | tf_op jit(solution)/shard_map/ppermute | solution.py:431

commit v2 on v1

--- a/solution.py
+++ b/solution.py
@@ -470,27 +470,23 @@
     sent = jnp.where(core == 0, halves[1], halves[0]).astype(BF16)
     total = kept + partner(sent, 1, 0).astype(F32)
 
-    steps = [[(0, 8)], [(0, 1)], [(8, 0)], [(0, 2)], [(0, 4)], [(2, 0)], [(4, 0)]]
+    steps = [[(0, 8)], [(0, 1), (8, 0), (8, 1)], [(0, 2)], [(0, 4)], [(2, 0)], [(4, 0)]]
     steps = [step for step in steps if all(a < n_lon and b < n_lat for a, b in step)]
-    total, (own0_b, below_b, corner_b, own1_b, side_b) = exchange(
-        total, steps[0], lambda *a: run_input_grad(*a, weights), (rows_b, gp, clq)
-    )
-    total, saved = exchange(
+    def far_step(rows_b, gp, clq, *halo):
+        return run_input_grad(rows_b, gp, clq, weights), run_forward_first(polar, x_a, halo, weights)
+
+    total, (pieces_b, saved) = exchange(total, steps[0], far_step, (rows_b, gp, clq, *halo))
+    own0_b, below_b, corner_b, own1_b, side_b = pieces_b
+    total, (own0_a, below, corner, own1_a, side) = exchange(
         total,
         steps[1],
-        lambda *halo: run_forward_first(polar, x_a, halo, weights),
-        halo,
-    )
-    total, (own0_a, below, corner, own1_a, side) = exchange(
-        total,
-        steps[2],
         lambda *a: run_forward_second(polar, a[:3], a[3:], weights),
         (*saved, below_b, corner_b, side_b),
     )
     below = shifted(below, 0, -1)
     corner = shifted(corner, -1, -1)
     side = shifted(side, -1, 0)
-    for step in steps[3:-1]:
+    for step in steps[2:-1]:
         total = exchange(total, step)[0]
     sent = total.astype(BF16)
     outs = run_add(x_a, cot, own0_a, own1_a, own0_b, own1_b, below, corner, side)

time: 89 us -> 89 us (level)
    ppermute x9 -> x10, waiting for transfers between devices: 13.3 us -> 9.74 us  [partner(): return lax.ppermute(block, ('lon', 'lat'), route)]
    ppermute x7, waiting for transfers between devices: 3.96 us -> 7.32 us  [shifted(): return lax.ppermute(block, ('lon', 'lat'), route)]
    ppermute x9 -> x10, starting transfers between devices: 15.7 us -> 19.1 us  [partner(): return lax.ppermute(block, ('lon', 'lat'), route)]
    ppermute x7, starting transfers between devices: 22.3 us -> 19.2 us  [shifted(): return lax.ppermute(block, ('lon', 'lat'), route)]
  transfers between devices with their start and end apart: 16 -> 17, of which waited for: 8 -> 7; matrix products, arithmetic and copies ran while one was open for 0% -> 0% of each run, Pallas kernels for 26% -> 26%
where the time goes in v2:
time: 89 us; the launch traced here: 88.9 us
  starting transfers between devices  38.3 us (43%)
  Pallas kernels  32.5 us (37%)
  waiting for transfers between devices  17.1 us (19%)
  between operations  0.9 us (1%)
    pallas_call x7, Pallas kernels, call(): pl.pallas_call(kernel, in_specs=[SMEM_SPEC] * len(scalars) + [VMEM_SPEC]...  26.7 us
    ppermute x7, starting transfers between devices, shifted(): return lax.ppermute(block, ('lon', 'lat'), route)  19.2 us
    ppermute x10, starting transfers between devices, partner(): return lax.ppermute(block, ('lon', 'lat'), route)  19.1 us
    ppermute x10, waiting for transfers between devices, partner(): return lax.ppermute(block, ('lon', 'lat'), route)  9.74 us
    ppermute x7, waiting for transfers between devices, shifted(): return lax.ppermute(block, ('lon', 'lat'), route)  7.32 us
    pallas_call x3, Pallas kernels, call_far(): pl.pallas_call(kernel, in_specs=[pl.BlockSpec(memory_space=pltpu.HBM)] *...  5.87 us
  transfers between devices with their start and end apart: 17, of which 7 were waited for; matrix products, arithmetic and copies ran while one was open for 0% of the time, Pallas kernels for 26%

profile of v2, /device:TPU:1, one launch (start us, length us, event | category | flops | bytes accessed | tf_op | source)
XLA Modules:
  0.0 88.9 jit_solution(12393017793086958725)
XLA Ops:
  0.6 1.3 %pack.1 = (bf16[1,108,1024]{2,1,0:T(8,128)(2,1)S(1)}, bf16[3,36,1024]{2,1,0:T(8,128)(2,1)S(1)}, bf16[3,36,1024]{2,1,0:T(8,128)(2,1)S(1)}) custom-call(bf16[12,12,2,1024]{3,2,1,0:T(2,128)(2,1)} %bitcast.12, bf16[12,12,2,1024]{3,2,1,0:T(2,128)(2,1)} %bitcast.18, bf16[12,12,2,1024]{3,2,1,0:T(2,128)(2,1)} %bitcast.14), custom_call_target="tpu_custom_call" | custom-call | flops 20000000000 | bytes 4000000 | tf_op jit(solution)/shard_map/pack/pallas_call | solution.py:333
  1.9 7.4 %collective-permute-start.3 = (bf16[1,108,1024]{2,1,0:T(8,128)(2,1)S(1)}, bf16[1,108,1024]{2,1,0:T(8,128)(2,1)S(1)}, u32[]{:S(2)}, u32[]{:S(2)}) collective-permute-start(bf16[1,108,1024]{2,1,0:T(8,128)(2,1)S(1)} %get-tuple-element.86), channel_id=1, source_target_pairs={{1,0},{2,1},{3,2},{4,3},{5,4},{6,5},{7,6},{8,7},{9,8},{10,9},{11,1... | collective-permute-start | bytes 663560 | tf_op jit(solution)/shard_map/ppermute | solution.py:423
  9.3 1.1 %collective-permute-start.1 = (bf16[3,36,1024]{2,1,0:T(8,128)(2,1)S(1)}, bf16[3,36,1024]{2,1,0:T(8,128)(2,1)S(1)}, u32[]{:S(2)}, u32[]{:S(2)}) collective-permute-start(bf16[3,36,1024]{2,1,0:T(8,128)(2,1)S(1)} %get-tuple-element.84), channel_id=1, source_target_pairs={{17,0},{18,1},{19,2},{20,3},{21,4},{22,5},{23,6},{24,7},{25,8},{26... | collective-permute-start | bytes 663560 | tf_op jit(solution)/shard_map/ppermute | solution.py:423
  10.4 3.6 %collective-permute-start.2 = (bf16[3,36,1024]{2,1,0:T(8,128)(2,1)S(1)}, bf16[3,36,1024]{2,1,0:T(8,128)(2,1)S(1)}, u32[]{:S(2)}, u32[]{:S(2)}) collective-permute-start(bf16[3,36,1024]{2,1,0:T(8,128)(2,1)S(1)} %get-tuple-element.85), channel_id=1, source_target_pairs={{16,0},{17,1},{18,2},{19,3},{20,4},{21,5},{22,6},{23,7},{24,8},{25... | collective-permute-start | bytes 663560 | tf_op jit(solution)/shard_map/ppermute | solution.py:423
  14.0 1.1 %pack_rest.1 = bf16[2,108,1024]{2,1,0:T(8,128)(2,1)S(1)} custom-call(bf16[12,12,2,1024]{3,2,1,0:T(2,128)(2,1)} %bitcast.19, bf16[12,12,2,1024]{3,2,1,0:T(2,128)(2,1)} %bitcast.15), custom_call_target="tpu_custom_call" | custom-call | flops 2000000000 | bytes 4000000 | tf_op jit(solution)/shard_map/pack_rest/pallas_call | solution.py:333
  15.1 1.0 %collective-permute-start = (bf16[2,108,1024]{2,1,0:T(8,128)(2,1)S(1)}, bf16[2,108,1024]{2,1,0:T(8,128)(2,1)S(1)}, u32[]{:S(2)}, u32[]{:S(2)}) collective-permute-start(bf16[2,108,1024]{2,1,0:T(8,128)(2,1)S(1)} %pack_rest.1), channel_id=1, source_target_pairs={{1,0},{2,1},{3,2},{4,3},{5,4},{6,5},{7,6},{8,7},{9,8},{10,9},{11,1... | collective-permute-start | bytes 1327112 | tf_op jit(solution)/shard_map/ppermute | solution.py:423
  16.1 0.0 copy-start
  16.1 0.0 copy-start.3
  16.1 0.0 copy-start.4
  16.1 0.0 copy-start.5
  16.1 0.0 copy-start.7
  16.1 3.5 %stage.1 = (bf16[1024,3072]{1,0:T(8,128)(2,1)S(1)}, bf16[1024,1024]{1,0:T(8,128)(2,1)S(1)}) custom-call(bf16[1024,3072]{1,0:T(8,128)(2,1)} %refs_0_, bf16[1024,1024]{1,0:T(8,128)(2,1)} %refs_1_), custom_call_target="tpu_custom_call" | custom-call | flops 3000000000 | bytes 4000000 | tf_op jit(solution)/shard_map/stage/pallas_call | solution.py:333
  19.6 0.0 collective-permute-done.3.below
  19.6 0.0 collective-permute-done.1.corner
  19.7 0.0 collective-permute-done.2.side
  19.7 0.0 copy-done
  19.7 0.0 copy-done.3
  19.7 0.0 copy-done.4
  19.7 0.0 copy-done.5
  19.7 0.0 copy-done.7
  19.7 0.0 copy-start.2
  19.7 0.0 copy-start.6
  19.7 6.5 %encode.1 = (f32[288,1024]{1,0:T(8,128)S(1)}, bf16[288,1024]{1,0:T(8,128)(2,1)S(1)}, bf16[8,288]{1,0:T(8,128)(2,1)S(1)}, bf16[288,3072]{1,0:T(8,128)(2,1)S(1)}, ...) custom-call(s32[1]{0:T(128)} %bitcast.3.polar_ref, ...), custom_call_target="tpu_custom_call" | custom-call | flops 7000000000 | bytes 4000000 | tf_op jit(solution)/shard_map/encode/pallas_call | solution.py:315
  26.2 2.5 %collective-permute-done.below = bf16[2,108,1024]{2,1,0:T(8,128)(2,1)S(1)} collective-permute-done((bf16[2,108,1024]{2,1,0:T(8,128)(2,1)S(1)}, bf16[2,108,1024]{2,1,0:T(8,128)(2,1)S(1)}, u32[]{:S(2)}, u32[]{:S(2)}) %collective-permute-start) | collective-permute-done | bytes 442400 | tf_op jit(solution)/shard_map/ppermute | solution.py:423
  28.7 0.0 copy-done.2
  28.7 0.0 copy-done.6
  28.7 0.0 copy-start.1
  28.7 7.1 %grads.1 = (bf16[288,3072]{1,0:T(8,128)(2,1)S(1)}, bf16[288,8]{1,0:T(8,128)(2,1)S(1)}, f32[4,48,256]{2,1,0:T(8,128)S(1)}) custom-call(bf16[12,12,2,1024]{3,2,1,0:T(2,128)(2,1)S(1)} %bitcast.20, bf16[2,108,1024]{2,1,0:T(8,128)(2,1)S(1)} %collective-permute-done.below, bf16[3,36,1024]{2,1,0:T(8,128)(2,1)S(1)} %collective-permute-done.1.corner, ...), custom_call_target="tpu_custom_call" | custom-call | flops 7000000000 | bytes 4000000 | tf_op jit(solution)/shard_map/grads/pallas_call | solution.py:315
  35.9 7.5 %collective-permute-start.4 = (bf16[2,48,256]{2,1,0:T(8,128)(2,1)S(1)}, bf16[2,48,256]{2,1,0:T(8,128)(2,1)S(1)}, u32[]{:S(2)}, u32[]{:S(2)}) collective-permute-start(bf16[2,48,256]{2,1,0:T(8,128)(2,1)S(1)} %select_convert_fusion), channel_id=1, source_target_pairs={{16,0},{17,1},{18,2},{19,3},{20,4},{21,5},{22,6},{23,7},{24,8},{25... | collective-permute-start | bytes 147464 | tf_op jit(solution)/shard_map/ppermute | solution.py:431
  43.4 0.9 collective-permute-done.4
  44.3 0.3 collective-permute-start.5
  44.6 0.0 copy-done.1
  44.6 3.3 %forward_first.1 = (bf16[288,1024]{1,0:T(8,128)(2,1)S(1)}, bf16[288,8]{1,0:T(8,128)(2,1)S(1)}, bf16[288,512]{1,0:T(8,128)(2,1)S(1)}) custom-call(s32[1]{0:T(128)} %bitcast.3.polar_ref, bf16[12,12,2,1024]{3,2,1,0:T(2,128)(2,1)S(1)} %bitcast.16, bf16[2,108,1024]{2,1,0:T(8,128)(2,1)S(1)} %collective-permute-done.below, ...), custom_call_target="tpu_custom_call" | custom-call | flops 4000000000 | bytes 4000000 | tf_op jit(solution)/shard_map/forward_first/pallas_call | solution.py:315
  47.9 2.4 %input_grad.1 = (bf16[72,1024]{1,0:T(8,128)(2,1)S(1)}, bf16[108,1024]{1,0:T(8,128)(2,1)S(1)}, bf16[36,1024]{1,0:T(8,128)(2,1)S(1)}, bf16[36,1024]{1,0:T(8,128)(2,1)S(1)}, bf16[36,1024]{1,0:T(8,128)(2,1)S(1)}) custom-call(f32[288,1024]{1,0:T(8,128)S(1)} %get-tuple-element.102.x_ref, f32[1,1024]{1,0:T(1,128)S(1)} %bitcast.30, ...), custom_call_target="tpu_custom_call" | custom-call | flops 3000000000 | bytes 4000000 | tf_op jit(solution)/shard_map/input_grad/pallas_call | solution.py:315
  50.4 1.1 %collective-permute-done.5 = bf16[2,48,256]{2,1,0:T(8,128)(2,1)S(1)} collective-permute-done((bf16[2,48,256]{2,1,0:T(8,128)(2,1)S(1)}, bf16[2,48,256]{2,1,0:T(8,128)(2,1)S(1)}, u32[]{:S(2)}, u32[]{:S(2)}) %collective-permute-start.5) | collective-permute-done | bytes 49184 | tf_op jit(solution)/shard_map/ppermute | solution.py:431
  51.5 0.1 collective-permute-start.6
  51.6 0.4 collective-permute-start.7
  51.9 3.5 %collective-permute-start.8 = (bf16[2,48,256]{2,1,0:T(8,128)(2,1)S(1)}, bf16[2,48,256]{2,1,0:T(8,128)(2,1)S(1)}, u32[]{:S(2)}, u32[]{:S(2)}) collective-permute-start(bf16[2,48,256]{2,1,0:T(8,128)(2,1)S(1)} %add_convert_fusion.5), channel_id=1, source_target_pairs={{129,0},{128,1},{131,2},{130,3},{133,4},{132,5},{135,6},{134,7},{1... | collective-permute-start | bytes 147464 | tf_op jit(solution)/shard_map/ppermute | solution.py:431
  55.4 4.4 %forward_second.1 = (bf16[1,72,1024]{2,1,0:T(8,128)(2,1)S(1)}, bf16[2,108,1024]{2,1,0:T(8,128)(2,1)S(1)}, bf16[2,36,1024]{2,1,0:T(8,128)(2,1)S(1)}, bf16[1,36,10...) custom-call(s32[1]{0:T(128)} %bitcast.3.polar_ref, bf16[288,1024]{1,0:T(8,128)(2,1)S(1)} %get-tuple-element.124.normed_ref, ...), custom_call_target="tpu_custom_call" | custom-call | flops 4000000000 | bytes 4000000 | tf_op jit(solution)/shard_map/forward_second/pallas_call | solution.py:315
  59.8 0.0 collective-permute-done.6
  59.8 0.0 collective-permute-done.7
  59.8 0.0 collective-permute-done.8
  59.9 0.1 collective-permute-start.9
  60.0 2.9 %collective-permute-done.9 = bf16[2,48,256]{2,1,0:T(8,128)(2,1)S(1)} collective-permute-done((bf16[2,48,256]{2,1,0:T(8,128)(2,1)S(1)}, bf16[2,48,256]{2,1,0:T(8,128)(2,1)S(1)}, u32[]{:S(2)}, u32[]{:S(2)}) %collective-permute-start.9) | collective-permute-done | bytes 49184 | tf_op jit(solution)/shard_map/ppermute | solution.py:431
  62.9 0.1 collective-permute-start.10
  63.0 0.1 collective-permute-start.13
  63.1 4.0 %collective-permute-done.10 = bf16[2,48,256]{2,1,0:T(8,128)(2,1)S(1)} collective-permute-done((bf16[2,48,256]{2,1,0:T(8,128)(2,1)S(1)}, bf16[2,48,256]{2,1,0:T(8,128)(2,1)S(1)}, u32[]{:S(2)}, u32[]{:S(2)}) %collective-permute-start.10) | collective-permute-done | bytes 49184 | tf_op jit(solution)/shard_map/ppermute | solution.py:431
  67.1 0.4 collective-permute-start.11
  67.5 4.3 %collective-permute-start.14 = (bf16[2,36,1024]{2,1,0:T(8,128)(2,1)S(1)}, bf16[2,36,1024]{2,1,0:T(8,128)(2,1)S(1)}, u32[]{:S(2)}, u32[]{:S(2)}) collective-permute-start(bf16[2,36,1024]{2,1,0:T(8,128)(2,1)S(1)} %get-tuple-element.143), channel_id=1, source_target_pairs={{255,0},{240,1},{241,2},{242,3},{243,4},{244,5},{245,6},{246,7},{2... | collective-permute-start | bytes 442376 | tf_op jit(solution)/shard_map/ppermute | solution.py:423
  71.8 1.7 %collective-permute-start.15 = (bf16[2,36,1024]{2,1,0:T(8,128)(2,1)S(1)}, bf16[2,36,1024]{2,1,0:T(8,128)(2,1)S(1)}, u32[]{:S(2)}, u32[]{:S(2)}) collective-permute-start(bf16[2,36,1024]{2,1,0:T(8,128)(2,1)S(1)} %get-tuple-element.144), channel_id=1, source_target_pairs={{240,0},{241,1},{242,2},{243,3},{244,4},{245,5},{246,6},{247,7},{2... | collective-permute-start | bytes 442376 | tf_op jit(solution)/shard_map/ppermute | solution.py:423
  73.5 0.0 collective-permute-done.11
  73.5 2.6 %collective-permute-start.12 = (bf16[2,48,256]{2,1,0:T(8,128)(2,1)S(1)}, bf16[2,48,256]{2,1,0:T(8,128)(2,1)S(1)}, u32[]{:S(2)}, u32[]{:S(2)}) collective-permute-start(bf16[2,48,256]{2,1,0:T(8,128)(2,1)S(1)} %add_convert_fusion.1), channel_id=1, source_target_pairs={{64,0},{65,1},{66,2},{67,3},{68,4},{69,5},{70,6},{71,7},{72,8},{73... | collective-permute-start | bytes 147464 | tf_op jit(solution)/shard_map/ppermute | solution.py:431
  76.1 4.8 %collective-permute-done.14.corner = bf16[2,36,1024]{2,1,0:T(8,128)(2,1)S(1)} collective-permute-done((bf16[2,36,1024]{2,1,0:T(8,128)(2,1)S(1)}, bf16[2,36,1024]{2,1,0:T(8,128)(2,1)S(1)}, u32[]{:S(2)}, u32[]{:S(2)}) %collective-permute-start.14) | collective-permute-done | bytes 147488 | tf_op jit(solution)/shard_map/ppermute | solution.py:423
  80.9 0.0 collective-permute-done.15.side
  80.9 0.0 collective-permute-done.13.below
  80.9 2.1 %add.46 = (bf16[12,12,2,1024]{3,2,1,0:T(2,128)(2,1)}, bf16[12,12,2,1024]{3,2,1,0:T(2,128)(2,1)}) custom-call(bf16[12,12,2,1024]{3,2,1,0:T(2,128)(2,1)S(1)} %bitcast.17, bf16[12,12,2,1024]{3,2,1,0:T(2,128)(2,1)S(1)} %bitcast.21, bf16[1,72,1024]{2,1,0:T(8,128)(2,1)S(1)} %get-tuple-element.138.own0_a, bf16[1,36,1024]{2,1,0:T(8,128)(2,1)S(1)} %get-tuple-element.139.own1_a, ...), custom_call_target="tpu_custom_call" | custom-call | flops 3000000000 | bytes 4000000 | tf_op jit(solution)/shard_map/add/pallas_call | solution.py:315
  83.0 0.0 collective-permute-done.12
  83.0 4.2 %collective-permute-start.16 = (bf16[2,48,256]{2,1,0:T(8,128)(2,1)S(1)}, bf16[2,48,256]{2,1,0:T(8,128)(2,1)S(1)}, u32[]{:S(2)}, u32[]{:S(2)}) collective-permute-start(bf16[2,48,256]{2,1,0:T(8,128)(2,1)S(1)} %add_convert_fusion.mine_ref), channel_id=1, source_target_pairs={{16,0},{17,1},{18,2},{19,3},{20,4},{21,5},{22,6},{23,7},{24,8},{25... | collective-permute-start | bytes 147464 | tf_op jit(solution)/shard_map/ppermute | solution.py:431
  87.2 0.9 collective-permute-done.16.other_ref
  88.1 0.8 clip.1
  (8 shorter events, 0.1 us)
Async XLA Ops:
  1.9 17.7 %collective-permute-start.3 = (bf16[1,108,1024]{2,1,0:T(8,128)(2,1)S(1)}, bf16[1,108,1024]{2,1,0:T(8,128)(2,1)S(1)}, u32[]{:S(2)}, u32[]{:S(2)}) collective-permute-start(bf16[1,108,1024]{2,1,0:T(8,128)(2,1)S(1)} %get-tuple-element.86), channel_id=1, source_target_pairs={{1,0},{2,1},{3,2},{4,3},{5,4},{6,5},{7,6},{8,7},{9,8},{10,9},{11,1... | collective-permute-start | bytes 663560 | tf_op jit(solution)/shard_map/ppermute | solution.py:423
  9.3 10.3 %collective-permute-start.1 = (bf16[3,36,1024]{2,1,0:T(8,128)(2,1)S(1)}, bf16[3,36,1024]{2,1,0:T(8,128)(2,1)S(1)}, u32[]{:S(2)}, u32[]{:S(2)}) collective-permute-start(bf16[3,36,1024]{2,1,0:T(8,128)(2,1)S(1)} %get-tuple-element.84), channel_id=1, source_target_pairs={{17,0},{18,1},{19,2},{20,3},{21,4},{22,5},{23,6},{24,7},{25,8},{26... | collective-permute-start | bytes 663560 | tf_op jit(solution)/shard_map/ppermute | solution.py:423
  10.4 9.2 %collective-permute-start.2 = (bf16[3,36,1024]{2,1,0:T(8,128)(2,1)S(1)}, bf16[3,36,1024]{2,1,0:T(8,128)(2,1)S(1)}, u32[]{:S(2)}, u32[]{:S(2)}) collective-permute-start(bf16[3,36,1024]{2,1,0:T(8,128)(2,1)S(1)} %get-tuple-element.85), channel_id=1, source_target_pairs={{16,0},{17,1},{18,2},{19,3},{20,4},{21,5},{22,6},{23,7},{24,8},{25... | collective-permute-start | bytes 663560 | tf_op jit(solution)/shard_map/ppermute | solution.py:423
  15.1 13.6 %collective-permute-start = (bf16[2,108,1024]{2,1,0:T(8,128)(2,1)S(1)}, bf16[2,108,1024]{2,1,0:T(8,128)(2,1)S(1)}, u32[]{:S(2)}, u32[]{:S(2)}) collective-permute-start(bf16[2,108,1024]{2,1,0:T(8,128)(2,1)S(1)} %pack_rest.1), channel_id=1, source_target_pairs={{1,0},{2,1},{3,2},{4,3},{5,4},{6,5},{7,6},{8,7},{9,8},{10,9},{11,1... | collective-permute-start | bytes 1327112 | tf_op jit(solution)/shard_map/ppermute | solution.py:423
  16.1 3.5 %copy-start = (bf16[2,12,12,1024]{3,0,2,1:T(2,128)(2,1)S(1)}, bf16[2,12,12,1024]{3,0,2,1:T(2,128)(2,1)}, u32[]{:S(2)}) copy-start(bf16[2,12,12,1024]{3,0,2,1:T(2,128)(2,1)} %param.11) | copy-start | bytes 1769476
  16.1 3.6 %copy-start.3 = (bf16[8,3072]{1,0:T(8,128)(2,1)S(1)}, bf16[8,3072]{1,0:T(8,128)(2,1)}, u32[]{:S(2)}) copy-start(bf16[8,3072]{1,0:T(8,128)(2,1)} %pu_ref.7) | copy-start | bytes 147460
  16.1 3.6 %copy-start.4 = (bf16[1024,8]{0,1:T(8,128)(2,1)S(1)}, bf16[1024,8]{0,1:T(8,128)(2,1)}, u32[]{:S(2)}) copy-start(bf16[1024,8]{0,1:T(8,128)(2,1)} %param.16) | copy-start | bytes 49156
  16.1 3.6 %copy-start.5 = (bf16[1024,8]{0,1:T(8,128)(2,1)S(1)}, bf16[1024,8]{0,1:T(8,128)(2,1)}, u32[]{:S(2)}) copy-start(bf16[1024,8]{0,1:T(8,128)(2,1)} %param.18) | copy-start | bytes 49156
  16.1 3.6 %copy-start.7 = (f32[1024]{0:T(1024)S(1)}, f32[1024]{0:T(1024)}, u32[]{:S(2)}) copy-start(f32[1024]{0:T(1024)} %param.13) | copy-start | bytes 12292
  19.7 9.0 %copy-start.2 = (bf16[2,12,12,1024]{3,0,2,1:T(2,128)(2,1)S(1)}, bf16[2,12,12,1024]{3,0,2,1:T(2,128)(2,1)}, u32[]{:S(2)}) copy-start(bf16[2,12,12,1024]{3,0,2,1:T(2,128)(2,1)} %param.12) | copy-start | bytes 1769476
  19.7 9.0 %copy-start.6 = (bf16[8,1024]{1,0:T(8,128)(2,1)S(1)}, bf16[8,1024]{1,0:T(8,128)(2,1)}, u32[]{:S(2)}) copy-start(bf16[8,1024]{1,0:T(8,128)(2,1)} %ou_ref.3) | copy-start | bytes 49156
  28.7 15.9 %copy-start.1 = (bf16[2,12,12,1024]{3,0,2,1:T(2,128)(2,1)S(1)}, bf16[2,12,12,1024]{3,0,2,1:T(2,128)(2,1)}, u32[]{:S(2)}) copy-start(bf16[2,12,12,1024]{3,0,2,1:T(2,128)(2,1)} %param.10) | copy-start | bytes 1769476
  35.9 8.4 %collective-permute-start.4 = (bf16[2,48,256]{2,1,0:T(8,128)(2,1)S(1)}, bf16[2,48,256]{2,1,0:T(8,128)(2,1)S(1)}, u32[]{:S(2)}, u32[]{:S(2)}) collective-permute-start(bf16[2,48,256]{2,1,0:T(8,128)(2,1)S(1)} %select_convert_fusion), channel_id=1, source_target_pairs={{16,0},{17,1},{18,2},{19,3},{20,4},{21,5},{22,6},{23,7},{24,8},{25... | collective-permute-start | bytes 147464 | tf_op jit(solution)/shard_map/ppermute | solution.py:431
  44.3 7.2 %collective-permute-start.5 = (bf16[2,48,256]{2,1,0:T(8,128)(2,1)S(1)}, bf16[2,48,256]{2,1,0:T(8,128)(2,1)S(1)}, u32[]{:S(2)}, u32[]{:S(2)}) collective-permute-start(bf16[2,48,256]{2,1,0:T(8,128)(2,1)S(1)} %add_convert_fusion.6), channel_id=1, source_target_pairs={{8,0},{9,1},{10,2},{11,3},{12,4},{13,5},{14,6},{15,7},{0,8},{1,9},... | collective-permute-start | bytes 147464 | tf_op jit(solution)/shard_map/ppermute | solution.py:431
  51.5 8.3 %collective-permute-start.6 = (bf16[2,48,256]{2,1,0:T(8,128)(2,1)S(1)}, bf16[2,48,256]{2,1,0:T(8,128)(2,1)S(1)}, u32[]{:S(2)}, u32[]{:S(2)}) collective-permute-start(bf16[2,48,256]{2,1,0:T(8,128)(2,1)S(1)} %add_convert_fusion.5), channel_id=1, source_target_pairs={{1,0},{0,1},{3,2},{2,3},{5,4},{4,5},{7,6},{6,7},{9,8},{8,9},{11,10... | collective-permute-start | bytes 147464 | tf_op jit(solution)/shard_map/ppermute | solution.py:431
  51.6 8.3 %collective-permute-start.7 = (bf16[2,48,256]{2,1,0:T(8,128)(2,1)S(1)}, bf16[2,48,256]{2,1,0:T(8,128)(2,1)S(1)}, u32[]{:S(2)}, u32[]{:S(2)}) collective-permute-start(bf16[2,48,256]{2,1,0:T(8,128)(2,1)S(1)} %add_convert_fusion.5), channel_id=1, source_target_pairs={{128,0},{129,1},{130,2},{131,3},{132,4},{133,5},{134,6},{135,7},{1... | collective-permute-start | bytes 147464 | tf_op jit(solution)/shard_map/ppermute | solution.py:431
  51.9 7.9 %collective-permute-start.8 = (bf16[2,48,256]{2,1,0:T(8,128)(2,1)S(1)}, bf16[2,48,256]{2,1,0:T(8,128)(2,1)S(1)}, u32[]{:S(2)}, u32[]{:S(2)}) collective-permute-start(bf16[2,48,256]{2,1,0:T(8,128)(2,1)S(1)} %add_convert_fusion.5), channel_id=1, source_target_pairs={{129,0},{128,1},{131,2},{130,3},{133,4},{132,5},{135,6},{134,7},{1... | collective-permute-start | bytes 147464 | tf_op jit(solution)/shard_map/ppermute | solution.py:431
  59.9 3.0 %collective-permute-start.9 = (bf16[2,48,256]{2,1,0:T(8,128)(2,1)S(1)}, bf16[2,48,256]{2,1,0:T(8,128)(2,1)S(1)}, u32[]{:S(2)}, u32[]{:S(2)}) collective-permute-start(bf16[2,48,256]{2,1,0:T(8,128)(2,1)S(1)} %add_convert_fusion.4), channel_id=1, source_target_pairs={{2,0},{3,1},{0,2},{1,3},{6,4},{7,5},{4,6},{5,7},{10,8},{11,9},{8,1... | collective-permute-start | bytes 147464 | tf_op jit(solution)/shard_map/ppermute | solution.py:431
  62.9 4.2 %collective-permute-start.10 = (bf16[2,48,256]{2,1,0:T(8,128)(2,1)S(1)}, bf16[2,48,256]{2,1,0:T(8,128)(2,1)S(1)}, u32[]{:S(2)}, u32[]{:S(2)}) collective-permute-start(bf16[2,48,256]{2,1,0:T(8,128)(2,1)S(1)} %add_convert_fusion.3), channel_id=1, source_target_pairs={{4,0},{5,1},{6,2},{7,3},{0,4},{1,5},{2,6},{3,7},{12,8},{13,9},{14,... | collective-permute-start | bytes 147464 | tf_op jit(solution)/shard_map/ppermute | solution.py:431
  63.0 17.9 %collective-permute-start.13 = (bf16[2,108,1024]{2,1,0:T(8,128)(2,1)S(1)}, bf16[2,108,1024]{2,1,0:T(8,128)(2,1)S(1)}, u32[]{:S(2)}, u32[]{:S(2)}) collective-permute-start(bf16[2,108,1024]{2,1,0:T(8,128)(2,1)S(1)} %get-tuple-element.142), channel_id=1, source_target_pairs={{15,0},{0,1},{1,2},{2,3},{3,4},{4,5},{5,6},{6,7},{7,8},{8,9},{9,10... | collective-permute-start | bytes 1327112 | tf_op jit(solution)/shard_map/ppermute | solution.py:423
  67.1 6.4 %collective-permute-start.11 = (bf16[2,48,256]{2,1,0:T(8,128)(2,1)S(1)}, bf16[2,48,256]{2,1,0:T(8,128)(2,1)S(1)}, u32[]{:S(2)}, u32[]{:S(2)}) collective-permute-start(bf16[2,48,256]{2,1,0:T(8,128)(2,1)S(1)} %add_convert_fusion.2), channel_id=1, source_target_pairs={{32,0},{33,1},{34,2},{35,3},{36,4},{37,5},{38,6},{39,7},{40,8},{41... | collective-permute-start | bytes 147464 | tf_op jit(solution)/shard_map/ppermute | solution.py:431
  67.5 13.4 %collective-permute-start.14 = (bf16[2,36,1024]{2,1,0:T(8,128)(2,1)S(1)}, bf16[2,36,1024]{2,1,0:T(8,128)(2,1)S(1)}, u32[]{:S(2)}, u32[]{:S(2)}) collective-permute-start(bf16[2,36,1024]{2,1,0:T(8,128)(2,1)S(1)} %get-tuple-element.143), channel_id=1, source_target_pairs={{255,0},{240,1},{241,2},{242,3},{243,4},{244,5},{245,6},{246,7},{2... | collective-permute-start | bytes 442376 | tf_op jit(solution)/shard_map/ppermute | solution.py:423
  71.8 9.1 %collective-permute-start.15 = (bf16[2,36,1024]{2,1,0:T(8,128)(2,1)S(1)}, bf16[2,36,1024]{2,1,0:T(8,128)(2,1)S(1)}, u32[]{:S(2)}, u32[]{:S(2)}) collective-permute-start(bf16[2,36,1024]{2,1,0:T(8,128)(2,1)S(1)} %get-tuple-element.144), channel_id=1, source_target_pairs={{240,0},{241,1},{242,2},{243,3},{244,4},{245,5},{246,6},{247,7},{2... | collective-permute-start | bytes 442376 | tf_op jit(solution)/shard_map/ppermute | solution.py:423
  73.5 9.5 %collective-permute-start.12 = (bf16[2,48,256]{2,1,0:T(8,128)(2,1)S(1)}, bf16[2,48,256]{2,1,0:T(8,128)(2,1)S(1)}, u32[]{:S(2)}, u32[]{:S(2)}) collective-permute-start(bf16[2,48,256]{2,1,0:T(8,128)(2,1)S(1)} %add_convert_fusion.1), channel_id=1, source_target_pairs={{64,0},{65,1},{66,2},{67,3},{68,4},{69,5},{70,6},{71,7},{72,8},{73... | collective-permute-start | bytes 147464 | tf_op jit(solution)/shard_map/ppermute | solution.py:431
  83.0 5.1 %collective-permute-start.16 = (bf16[2,48,256]{2,1,0:T(8,128)(2,1)S(1)}, bf16[2,48,256]{2,1,0:T(8,128)(2,1)S(1)}, u32[]{:S(2)}, u32[]{:S(2)}) collective-permute-start(bf16[2,48,256]{2,1,0:T(8,128)(2,1)S(1)} %add_convert_fusion.mine_ref), channel_id=1, source_target_pairs={{16,0},{17,1},{18,2},{19,3},{20,4},{21,5},{22,6},{23,7},{24,8},{25... | collective-permute-start | bytes 147464 | tf_op jit(solution)/shard_map/ppermute | solution.py:431
